TPU v7x, 256 devices: a whole 4x4x8 slice. The times are simulated.
256 devices in a mesh: ta: 4 (over x), gy: 8 (over y, core), gx: 8 (over z).
Axes of the slice: x: 4, y: 4, z: 8, core: 2. Of those that a mesh axis runs over, the one named last changes fastest.
Arguments:
- latents: bfloat16 [8, 128, 128, 256], P('ta', 'gy', 'gx'), may hold values from -32 to 32
- gain_one: float32 [256], replicated, may hold values from 0.1 to 1.9
- shift_one: float32 [256], replicated, may hold values from -3 to 3
- weight_one: bfloat16 [3, 3, 3, 256, 256], replicated, may hold values from -0.078125 to 0.078125
- bias_one: float32 [256], replicated, may hold values from -3 to 3
- gain_two: float32 [256], replicated, may hold values from 0.1 to 1.9
- shift_two: float32 [256], replicated, may hold values from -3 to 3
- weight_two: bfloat16 [3, 3, 3, 256, 128], replicated, may hold values from -0.078125 to 0.078125
- weight_skip: bfloat16 [256, 128], replicated, may hold values from -0.375 to 0.375
- bias_two: float32 [128], replicated, may hold values from -3 to 3
Outputs:
- decoded: bfloat16 [8, 256, 256, 128], P('ta', 'gy', 'gx')
All inputs are finite; a program needn't handle non-finite values.
Results may differ from a plain program's by a relative error of at most 0.0056.
Values may be sent and summed in bfloat16 or wider, within the bound.
A program may use at most 64 MiB of HBM per device.

v0:
```python
import jax
import jax.numpy as jnp
from jax import lax
from jax.sharding import PartitionSpec as P

GROUPS = 32


EPS = 1e-06


def prefix_2(array, axis, combine, identity):
    peers, place = (lax.axis_size(axis), lax.axis_index(axis))
    everything = lax.all_gather(array, axis)
    start = jnp.broadcast_to(jnp.asarray(identity, array.dtype), array.shape)

    def hop(k, before):
        reached = k < place
        new = combine(before, everything[k])
        return jnp.where(reached, new, before)

    return lax.fori_loop(0, peers, hop, start)


def shifted(value, axis, steps):
    count = lax.axis_size(axis)
    leading, last = (max(0, -steps), min(count, count - steps))
    return lax.ppermute(value, axis, [(source, source + steps) for source in range(leading, last)])


def padded_2(block, sides, width):
    for axis, dim in sides:
        count = lax.axis_size(axis)
        forward = [(i, i + 1) for i in range(count - 1)]
        backward = [(target, source) for source, target in forward]
        low = lax.ppermute(
            lax.slice_in_dim(block, block.shape[dim] - width, None, axis=dim), axis, forward
        )
        high = lax.ppermute(lax.slice_in_dim(block, 0, width, axis=dim), axis, backward)
        block = jnp.concatenate([low, block, high], axis=dim)
    return block


def frame_sums(values):
    wide = values.astype(jnp.float32)
    sums = jnp.stack([jnp.sum(wide, axis=(1, 2)), jnp.sum(wide * wide, axis=(1, 2))], axis=1)
    return sums.reshape(values.shape[0], 2, GROUPS, -1).sum(-1)


def cumulative(local):
    frames = local.shape[0]
    start = lax.axis_index("ta") * frames
    grid = lax.psum(local, ("gy", "gx"))
    prefix = prefix_2(
        jnp.sum(grid, axis=0),
        "ta",
        lambda early, late: early + late,
        jnp.zeros(grid.shape[1:], jnp.float32),
    )
    return (prefix[None] + jnp.cumsum(grid, axis=0), start)


def frame_steps(start, frames):
    return start.astype(jnp.float32) + jnp.arange(frames, dtype=jnp.float32) + 1.0


def normalize(values, running, steps, gain, shift, area):
    width = values.shape[3] // GROUPS
    count = steps * (area * width)
    mean = running[:, 0] / count[:, None]
    var = running[:, 1] / count[:, None] - mean * mean
    inv = lax.rsqrt(var + EPS)
    scale = jnp.repeat(inv, width, axis=1) * gain[None, :]
    offset = shift[None, :] - jnp.repeat(mean, width, axis=1) * scale
    wide = values.astype(jnp.float32) * scale[:, None, None, :] + offset[:, None, None, :]
    return jax.nn.silu(wide).astype(jnp.bfloat16)


def edge_fix(padded):
    row_index = lax.axis_index("gy")
    row_count = lax.axis_size("gy")
    top = jnp.where(row_index == 0, padded[:, 1:2], padded[:, 0:1])
    bottom = jnp.where(row_index == row_count - 1, padded[:, -2:-1], padded[:, -1:])
    padded = jnp.concatenate([top, padded[:, 1:-1], bottom], axis=1)
    col_index = lax.axis_index("gx")
    col_count = lax.axis_size("gx")
    left = jnp.where(col_index == 0, padded[:, :, 1:2], padded[:, :, 0:1])
    right = jnp.where(col_index == col_count - 1, padded[:, :, -2:-1], padded[:, :, -1:])
    return jnp.concatenate([left, padded[:, :, 1:-1], right], axis=2)


def pad_block(normed):
    first_span = lax.axis_index("ta") == 0
    cache = shifted(normed, "ta", 1)
    cache = jnp.where(first_span, jnp.broadcast_to(normed[:1], normed.shape), cache)
    joined = jnp.concatenate([cache, normed], axis=0)
    padded = padded_2(joined, (("gy", 1), ("gx", 2)), 1)
    return edge_fix(padded)


def convolve(padded, kernel, frames, rows, cols):
    total = jnp.zeros((frames * rows * cols, kernel.shape[4]), jnp.float32)
    for a in range(3):
        for b in range(3):
            for c in range(3):
                piece = padded[a : a + frames, b : b + rows, c : c + cols].reshape(
                    frames * rows * cols, -1
                )
                total = total + jnp.dot(piece, kernel[a, b, c], preferred_element_type=jnp.float32)
    return total


def on_device(
    latents,
    gain_one,
    shift_one,
    weight_one,
    bias_one,
    gain_two,
    shift_two,
    weight_two,
    weight_skip,
    bias_two,
):
    frames, rows, cols, channels = latents.shape
    area = rows * cols * lax.axis_size("gy") * lax.axis_size("gx")
    running_one, start = cumulative(frame_sums(latents))
    first = normalize(latents, running_one, frame_steps(start, frames), gain_one, shift_one, area)
    conv_one = convolve(pad_block(first), weight_one, frames, rows, cols).reshape(latents.shape)
    block_out = (latents.astype(jnp.float32) + conv_one + bias_one).astype(jnp.bfloat16)
    running_two, start = cumulative(4.0 * frame_sums(block_out))
    upsampled = jnp.repeat(jnp.repeat(block_out, 2, axis=1), 2, axis=2)
    second = normalize(
        upsampled, running_two, frame_steps(start, frames), gain_two, shift_two, 4 * area
    )
    padded_two = pad_block(second)
    conv_part = convolve(padded_two, weight_two, frames, 2 * rows, 2 * cols)
    skip_part = jnp.dot(
        upsampled.reshape(-1, channels), weight_skip, preferred_element_type=jnp.float32
    )
    decoded = conv_part + skip_part + bias_two
    return decoded.reshape(frames, 2 * rows, 2 * cols, -1).astype(jnp.bfloat16)


def solution(mesh):
    in_specs = (P("ta", "gy", "gx", None), P(), P(), P(), P(), P(), P(), P(), P(), P())
    out_specs = P("ta", "gy", "gx", None)
    return jax.shard_map(
        on_device, mesh=mesh, in_specs=in_specs, out_specs=out_specs, check_vma=False
    )
```

profile of v0, /device:TPU:1, one launch (start us, length us, event | category | flops | bytes accessed | tf_op | source)
XLA Modules:
  0.0 382.2 jit_solution(14292720236409660031)
XLA Ops:
  0.0 1.1 convert_reduce_fusion
  1.4 124.3 %psum.14 = f32[2,2,32]{2,1,0:T(2,128)S(1)} all-reduce(f32[2,2,32]{2,1,0:T(2,128)S(1)} %maximum_reduce_fusion), channel_id=1, replica_groups=mesh['ta'=4,'gy'=8,'gx'=8] {'gy','gx'}, use_global_device_ids=true, to_apply=%region_3.0 | all-reduce | flops 128 | bytes 1024 | tf_op jit(solution)/shard_map/psum | solution.py:53
  125.7 8.0 %all-gather.2 = f32[4,2,32]{2,1,0:T(2,128)S(1)} all-gather(f32[1,2,32]{2,1,0:T(2,128)S(1)} %bitcast.353), channel_id=2, replica_groups=mesh['ta'=4,'gy'=8,'gx'=8] {'ta'}, dimensions={0}, use_global_device_ids=true | all-gather | bytes 1280 | tf_op jit(solution)/shard_map/all_gather | solution.py:14
  134.3 0.7 multiply_subtract_fusion.1
  135.0 1.1 fusion.32
  136.1 1.3 collective-permute-start
  137.5 3.3 collective-permute-done
  140.8 1.9 collective-permute-start.1
  142.7 12.8 %collective-permute-start.2 = (bf16[4,1,16,256]{3,2,1,0:T(8,128)(2,1)S(1)}, bf16[4,1,16,256]{3,2,1,0:T(8,128)(2,1)S(1)}, u32[]{:S(2)}, u32[]{:S(2)}) collective-permute-start(bf16[4,1,16,256]{3,2,1,0:T(8,128)(2,1)S(1)} %get-tuple-element.289), channel_id=1, source_target_pairs={{8,0},{16,8},{24,16},{32,24},{40,32},{48,40},{56,48},{9,1},{17,9},... | collective-permute-start | bytes 98312 | tf_op jit(solution)/shard_map/ppermute | solution.py:39
  155.5 0.8 collective-permute-done.2
  156.5 1.3 collective-permute-start.3
  157.8 1.3 collective-permute-start.4
  159.4 3.5 collective-permute-done.4
  162.9 0.6 pad_maximum_fusion.7
  164.6 0.6 pad_maximum_fusion.11
  165.2 0.8 pad_maximum_fusion.9
  166.0 0.6 copy-done.1
  173.5 116.8 %psum.15 = f32[2,2,32]{2,1,0:T(2,128)S(1)} all-reduce(f32[2,2,32]{2,1,0:T(2,128)S(1)} %broadcast_multiply_fusion.1), channel_id=1, replica_groups=mesh['ta'=4,'gy'=8,'gx'=8] {'gy','gx'}, use_global_device_ids=true, to_apply=%region_11.12 | all-reduce | flops 128 | bytes 1024 | tf_op jit(solution)/shard_map/psum | solution.py:53
  290.3 7.8 %all-gather.3 = f32[4,2,32]{2,1,0:T(2,128)S(1)} all-gather(f32[1,2,32]{2,1,0:T(2,128)S(1)} %bitcast.352), channel_id=3, replica_groups=mesh['ta'=4,'gy'=8,'gx'=8] {'ta'}, dimensions={0}, use_global_device_ids=true | all-gather | bytes 1280 | tf_op jit(solution)/shard_map/all_gather | solution.py:14
  298.8 1.1 broadcast_in_dim.27
  299.9 2.5 convert_element_type.53
  302.4 2.3 multiply_convert_fusion
  304.7 2.5 collective-permute-start.5
  307.2 11.9 %collective-permute-done.5 = bf16[2,32,32,256]{3,2,1,0:T(8,128)(2,1)S(1)} collective-permute-done((bf16[2,32,32,256]{3,2,1,0:T(8,128)(2,1)S(1)}, bf16[2,32,32,256]{3,2,1,0:T(8,128)(2,1)S(1)}, u32[]{:S(2)}, u32[]{:S(2)}) %collective-permute-start.5) | collective-permute-done | bytes 1048608 | tf_op jit(solution)/shard_map/ppermute | solution.py:28
  319.3 1.9 collective-permute-start.6
  321.2 12.6 %collective-permute-start.7 = (bf16[4,1,32,256]{3,2,1,0:T(8,128)(2,1)S(1)}, bf16[4,1,32,256]{3,2,1,0:T(8,128)(2,1)S(1)}, u32[]{:S(2)}, u32[]{:S(2)}) collective-permute-start(bf16[4,1,32,256]{3,2,1,0:T(8,128)(2,1)S(1)} %get-tuple-element.256), channel_id=1, source_target_pairs={{8,0},{16,8},{24,16},{32,24},{40,32},{48,40},{56,48},{9,1},{17,9},... | collective-permute-start | bytes 196616 | tf_op jit(solution)/shard_map/ppermute | solution.py:39
  333.8 2.1 broadcast_in_dim.60
  335.9 1.5 reshape_reshape.3
  337.6 3.6 collective-permute-start.8
  341.2 1.3 collective-permute-start.9
  342.6 1.8 collective-permute-done.8
  344.4 4.3 %collective-permute-done.9 = bf16[4,34,1,256]{3,2,1,0:T(2,128)(2,1)S(1)} collective-permute-done((bf16[4,34,1,256]{3,2,1,0:T(2,128)(2,1)S(1)}, bf16[4,34,1,256]{3,2,1,0:T(2,128)(2,1)S(1)}, u32[]{:S(2)}, u32[]{:S(2)}) %collective-permute-start.9) | collective-permute-done | bytes 69664 | tf_op jit(solution)/shard_map/ppermute | solution.py:39
  348.7 2.0 pad_maximum_fusion
  351.0 3.4 pad_maximum_fusion.3
  355.2 1.2 slice.687
  356.4 6.3 %pad_maximum_fusion.4 = (bf16[2,32,32,256]{3,2,1,0:T(8,128)(2,1)S(1)}, bf16[2,32,32,256]{3,2,1,0:T(8,128)(2,1)S(1)}, bf16[2,32,32,256]{3,2,1,0:T(8,128)(2,1)S(1)...) fusion(bf16[4,34,32,256]{3,2,1,0:T(8,128)(2,1)S(1)} %slice.687,, ...), kind=kLoop, calls=%fused_computation.156 | loop fusion | flops 18874368 | bytes 11735040 | tf_op jit(solution)/shard_map/concatenate | solution.py:89
  362.7 6.1 %pad_maximum_fusion.2 = (bf16[2,32,32,256]{3,2,1,0:T(8,128)(2,1)S(1)}, bf16[2,32,32,256]{3,2,1,0:T(8,128)(2,1)S(1)}, bf16[2,32,32,256]{3,2,1,0:T(8,128)(2,1)S(1)...) fusion(bf16[4,34,1,256]{3,2,1,0:T(2,128)(2,1)S(1)} %get-tuple-e, ...), kind=kLoop, calls=%fused_computation.154 | loop fusion | flops 18874368 | bytes 11735040 | tf_op jit(solution)/shard_map/concatenate | solution.py:89
  369.3 0.4 fusion.128
  369.7 0.4 convolution_add_fusion.25
  370.2 0.4 convolution_add_fusion.24
  370.6 0.4 convolution_add_fusion.23
  371.0 0.5 fusion.1
  371.5 0.4 convolution_add_fusion.21
  372.0 0.4 convolution_add_fusion.20
  372.4 0.4 convolution_add_fusion.19
  372.8 0.4 convolution_add_fusion.18
  373.3 0.4 convolution_add_fusion.17
  373.7 0.4 convolution_add_fusion.16
  374.1 0.4 convolution_add_fusion.15
  374.6 0.5 convolution_add_fusion.14
  375.0 0.4 convolution_add_fusion.13
  375.5 0.4 convolution_add_fusion.12
  375.9 0.4 convolution_add_fusion.11
  376.4 0.4 convolution_add_fusion.10
  376.8 0.4 convolution_add_fusion.9
  377.2 0.4 convolution_add_fusion.8
  377.7 0.4 convolution_add_fusion.7
  378.1 0.4 convolution_add_fusion.6
  378.6 0.4 convolution_add_fusion.5
  379.0 0.4 convolution_add_fusion.4
  379.4 0.4 convolution_add_fusion.3
  379.9 0.4 convolution_add_fusion.2
  380.3 0.4 convolution_add_fusion.1
  381.0 1.2 fusion.2
  (112 shorter events, 12.1 us)
Async XLA Ops:
  0.0 380.7 %copy-start = (bf16[256,128]{1,0:T(8,128)(2,1)S(1)}, bf16[256,128]{1,0:T(8,128)(2,1)}, u32[]{:S(2)}) copy-start(bf16[256,128]{1,0:T(8,128)(2,1)} %param.22) | copy-start | bytes 196612
  136.1 4.6 %collective-permute-start = (bf16[2,16,16,256]{3,2,1,0:T(8,128)(2,1)S(1)}, bf16[2,16,16,256]{3,2,1,0:T(8,128)(2,1)S(1)}, u32[]{:S(2)}, u32[]{:S(2)}) collective-permute-start(bf16[2,16,16,256]{3,2,1,0:T(8,128)(2,1)S(1)} %fusion.32), channel_id=1, source_target_pairs={{0,64},{64,128},{128,192},{1,65},{65,129},{129,193},{2,66},{66,130... | collective-permute-start | bytes 786440 | tf_op jit(solution)/shard_map/ppermute | solution.py:28
  140.8 14.8 %collective-permute-start.1 = (bf16[4,1,16,256]{3,2,1,0:T(8,128)(2,1)S(1)}, bf16[4,1,16,256]{3,2,1,0:T(8,128)(2,1)S(1)}, u32[]{:S(2)}, u32[]{:S(2)}) collective-permute-start(bf16[4,1,16,256]{3,2,1,0:T(8,128)(2,1)S(1)} %get-tuple-element.288), channel_id=1, source_target_pairs={{0,8},{8,16},{16,24},{24,32},{32,40},{40,48},{48,56},{1,9},{9,17},... | collective-permute-start | bytes 98312 | tf_op jit(solution)/shard_map/ppermute | solution.py:36
  142.7 13.6 %collective-permute-start.2 = (bf16[4,1,16,256]{3,2,1,0:T(8,128)(2,1)S(1)}, bf16[4,1,16,256]{3,2,1,0:T(8,128)(2,1)S(1)}, u32[]{:S(2)}, u32[]{:S(2)}) collective-permute-start(bf16[4,1,16,256]{3,2,1,0:T(8,128)(2,1)S(1)} %get-tuple-element.289), channel_id=1, source_target_pairs={{8,0},{16,8},{24,16},{32,24},{40,32},{48,40},{56,48},{9,1},{17,9},... | collective-permute-start | bytes 98312 | tf_op jit(solution)/shard_map/ppermute | solution.py:39
  156.5 2.9 collective-permute-start.3
  157.8 5.1 %collective-permute-start.4 = (bf16[4,18,1,256]{3,2,1,0:T(2,128)(2,1)S(1)}, bf16[4,18,1,256]{3,2,1,0:T(2,128)(2,1)S(1)}, u32[]{:S(2)}, u32[]{:S(2)}) collective-permute-start(bf16[4,18,1,256]{3,2,1,0:T(2,128)(2,1)S(1)} %get-tuple-element.287), channel_id=1, source_target_pairs={{1,0},{2,1},{3,2},{4,3},{5,4},{6,5},{7,6},{9,8},{10,9},{11,10},{12... | collective-permute-start | bytes 110600 | tf_op jit(solution)/shard_map/ppermute | solution.py:39
  164.5 2.0 copy-start.1
  172.1 1.0 copy-start.2
  172.1 0.9 copy-start.4
  299.8 2.5 copy-start.5
  299.9 2.5 copy-start.6
  304.7 14.5 %collective-permute-start.5 = (bf16[2,32,32,256]{3,2,1,0:T(8,128)(2,1)S(1)}, bf16[2,32,32,256]{3,2,1,0:T(8,128)(2,1)S(1)}, u32[]{:S(2)}, u32[]{:S(2)}) collective-permute-start(bf16[2,32,32,256]{3,2,1,0:T(8,128)(2,1)S(1)} %multiply_convert_fusion), channel_id=1, source_target_pairs={{0,64},{64,128},{128,192},{1,65},{65,129},{129,193},{2,66},{66,130... | collective-permute-start | bytes 3145736 | tf_op jit(solution)/shard_map/ppermute | solution.py:28
  319.3 18.1 %collective-permute-start.6 = (bf16[4,1,32,256]{3,2,1,0:T(8,128)(2,1)S(1)}, bf16[4,1,32,256]{3,2,1,0:T(8,128)(2,1)S(1)}, u32[]{:S(2)}, u32[]{:S(2)}) collective-permute-start(bf16[4,1,32,256]{3,2,1,0:T(8,128)(2,1)S(1)} %get-tuple-element.255), channel_id=1, source_target_pairs={{0,8},{8,16},{16,24},{24,32},{32,40},{40,48},{48,56},{1,9},{9,17},... | collective-permute-start | bytes 196616 | tf_op jit(solution)/shard_map/ppermute | solution.py:36
  321.2 16.2 %collective-permute-start.7 = (bf16[4,1,32,256]{3,2,1,0:T(8,128)(2,1)S(1)}, bf16[4,1,32,256]{3,2,1,0:T(8,128)(2,1)S(1)}, u32[]{:S(2)}, u32[]{:S(2)}) collective-permute-start(bf16[4,1,32,256]{3,2,1,0:T(8,128)(2,1)S(1)} %get-tuple-element.256), channel_id=1, source_target_pairs={{8,0},{16,8},{24,16},{32,24},{40,32},{48,40},{56,48},{9,1},{17,9},... | collective-permute-start | bytes 196616 | tf_op jit(solution)/shard_map/ppermute | solution.py:39
  337.6 6.8 %collective-permute-start.8 = (bf16[4,34,1,256]{3,2,1,0:T(2,128)(2,1)S(1)}, bf16[4,34,1,256]{3,2,1,0:T(2,128)(2,1)S(1)}, u32[]{:S(2)}, u32[]{:S(2)}) collective-permute-start(bf16[4,34,1,256]{3,2,1,0:T(2,128)(2,1)S(1)} %get-tuple-element.253), channel_id=1, source_target_pairs={{0,1},{1,2},{2,3},{3,4},{4,5},{5,6},{6,7},{8,9},{9,10},{10,11},{11... | collective-permute-start | bytes 208904 | tf_op jit(solution)/shard_map/ppermute | solution.py:36
  341.2 7.5 %collective-permute-start.9 = (bf16[4,34,1,256]{3,2,1,0:T(2,128)(2,1)S(1)}, bf16[4,34,1,256]{3,2,1,0:T(2,128)(2,1)S(1)}, u32[]{:S(2)}, u32[]{:S(2)}) collective-permute-start(bf16[4,34,1,256]{3,2,1,0:T(2,128)(2,1)S(1)} %get-tuple-element.254), channel_id=1, source_target_pairs={{1,0},{2,1},{3,2},{4,3},{5,4},{6,5},{7,6},{9,8},{10,9},{11,10},{12... | collective-permute-start | bytes 208904 | tf_op jit(solution)/shard_map/ppermute | solution.py:39
  362.7 6.1 %copy-start.3 = (bf16[3,3,3,256,128]{4,3,2,1,0:T(8,128)(2,1)S(1)}, bf16[3,3,3,256,128]{4,3,2,1,0:T(8,128)(2,1)}, u32[]{:S(2)}) copy-start(bf16[3,3,3,256,128]{4,3,2,1,0:T(8,128)(2,1)} %param.21) | copy-start | bytes 5308420
  380.3 0.7 copy-start.7
where the time goes:
time: 383 us; the launch traced here: 382 us
  blocking collectives  257 us (67%)
  starting transfers between devices  40.5 us (11%)
  other arithmetic  27.7 us (7%)
  waiting for transfers between devices  25.8 us (7%)
  matrix products  19.1 us (5%)
  local copies, waits for them, and re-layouts  11.3 us (3%)
    psum x2, blocking collectives, cumulative(): grid = lax.psum(local, ('gy', 'gx'))  241 us
    ppermute x4, starting transfers between devices, padded_2(): lax.ppermute(lax.slice_in_dim(block, 0, width, axis=dim), axis, backward)  28 us
    dot_general x54, matrix products, convolve(): jnp.dot(piece, kernel[a, b, c], preferred_element_type=jnp.float32)  17.8 us
    all_gather x2, blocking collectives, prefix_2(): everything = lax.all_gather(array, axis)  15.8 us
    ppermute x2, waiting for transfers between devices, shifted(): lax.ppermute(value, axis, [(source, source + steps) for source in range(l...  15.2 us
    concatenate x4, other arithmetic, edge_fix(): return jnp.concatenate([left, padded[:, :, 1:-1], right], axis=2)  13.8 us
    ppermute x4, starting transfers between devices, padded_2(): lax.ppermute(lax.slice_in_dim(block, block.shape[dim] - width, None, axis...  8.72 us
    ppermute x4, waiting for transfers between devices, padded_2(): lax.ppermute(lax.slice_in_dim(block, 0, width, axis=dim), axis, backward)  8.56 us
  transfers between devices with their start and end apart: 10, of which 7 were waited for; matrix products, arithmetic and copies ran while one was open for 1% of the time, Pallas kernels for 0%

commit v1 on v0

v1 whole, which is shorter than its diff:
```python
import jax
import jax.numpy as jnp
from jax import lax
from jax.experimental import pallas as pl
from jax.experimental.pallas import tpu as pltpu
from jax.sharding import PartitionSpec as P

MESH = pl.DeviceIdType.MESH
F32 = jnp.float32
BF16 = jnp.bfloat16
EPS = 1e-06

NTA, NCHIP, NGX = 4, 4, 8
NGY = 2 * NCHIP
ROWS, COLS, CH, CO = 16, 16, 256, 128
AREA = float(NGY * ROWS * NGX * COLS * (CH // 32))

STEP_A = [(c, k) for k in (4, 3, -3, 2, -2, 1, -1, 0) for c in (1, 0) if (c, k) != (0, 0)]
STEP_B = [(j, k) for j in range(NTA) for k in range(NCHIP) if (j, k) != (0, 0)]
STEP_B_ORDER = sorted(STEP_B, key=lambda p: -(min(p[0], NTA - p[0]) + min(p[1], NCHIP - p[1])))

PIECES = [
    (-1, 0, "row", 1, ROWS + 1),
    (1, 0, "row", ROWS, 0),
    (0, -1, "col", 0, 1),
    (0, 1, "col", 1, 0),
    (-1, -1, "corner", 0, 3),
    (-1, 1, "corner", 1, 2),
    (1, -1, "corner", 2, 1),
    (1, 1, "corner", 3, 0),
]


def wrap(value, size):
    return lax.rem(value + size, size)


def kernel(
    lat, w1h, w2h, wsh, g1h, s1h, b1h, g2h, s2h, b2h, out,
    buf, colp, colr, cb, cr, wide, xs, hal, sums, red, sc, w1, w2, we, ws, prm, b2,
    acc1, acc2, skip, tmp, ob,
    msg, da, db, ssem, rsem, ssem_a, rsem_a, ssem_b, rsem_b, lsem, osem,
):
    t = lax.axis_index("ta")
    gy = lax.axis_index("gy")
    gx = lax.axis_index("gx")
    chip, core = gy // 2, lax.rem(gy, 2)

    def at(dt, dy, dx):
        return (wrap(t + dt, NTA), wrap(gy + dy, NGY), wrap(gx + dx, NGX))

    def on_line(c, k):
        return (t, chip * 2 + (1 - core if c else core), wrap(gx + k, NGX))

    def on_plane(j, k):
        return (wrap(t + j, NTA), wrap(chip + k, NCHIP) * 2 + core, gx)

    ready = pltpu.get_barrier_semaphore()
    senders = [on_line(c, k) for c, k in STEP_A] + [on_plane(j, k) for j, k in STEP_B]
    senders += [at(0, dy, dx) for dy, dx, _, _, _ in PIECES]
    senders += [at(-1, 0, 0)] + [at(-1, dy, dx) for dy, dx, _, _, _ in PIECES]
    load_lat = pltpu.make_async_copy(lat, buf.at[0, 2:4, 1 : ROWS + 1], lsem.at[0])
    load_lat.start()
    for device in senders:
        pl.semaphore_signal(ready, inc=1, device_id=device, device_id_type=MESH)
    loads = [
        pltpu.make_async_copy(src, dst, lsem.at[i + 1])
        for i, (src, dst) in enumerate(
            [(w2h, w2), (wsh, ws), (g1h, prm.at[0]), (s1h, prm.at[1]), (b1h, prm.at[2]),
             (g2h, prm.at[3]), (s2h, prm.at[4]), (b2h, b2), (w1h, w1)]
        )
    ]
    for load in loads:
        load.start()

    lane = lax.broadcasted_iota(jnp.int32, (8, 128), 1)
    pick = lax.rem(lane, 8) == lax.broadcasted_iota(jnp.int32, (8, 128), 0)
    row_id = lax.broadcasted_iota(jnp.int32, (COLS, 128), 0)

    def group_sum(v):
        for d in (1, 2, 4):
            v = v + jnp.where((lane & d) != 0, pltpu.roll(v, d, 1), pltpu.roll(v, 128 - d, 1))
        return v

    def compact(v):
        return jnp.sum(jnp.where(pick, group_sum(v), 0.0), axis=0, keepdims=True)

    def expand(row):
        return group_sum(jnp.where(pick, jnp.broadcast_to(row, (8, 128)), 0.0))

    def take_in(stage, block):
        for f in range(2):

            def step(r, carry):
                s, q = carry
                v = block(f, r)
                place = pl.ds(pl.multiple_of((f * ROWS + r) * COLS, COLS), COLS)
                for h in range(2):
                    wide[h, place] = v[:, h * 128 : h * 128 + 128]
                return s + v, q + v * v

            zero = jnp.zeros((COLS, CH), F32)
            s, q = lax.fori_loop(0, ROWS, step, (zero, zero), unroll=4)
            s = jnp.sum(s, axis=0, keepdims=True)
            q = jnp.sum(q, axis=0, keepdims=True)
            for h in range(2):
                lanes = slice(h * 128, h * 128 + 128)
                sums[f * 2 + h : f * 2 + h + 1] = s[:, lanes]
                sums[4 + f * 2 + h : 5 + f * 2 + h] = q[:, lanes]

    def edges(stage):
        for f in range(2):
            base = f * ROWS * COLS
            for side, c in ((0, 0), (1, COLS - 1)):
                for h in range(2):
                    col = wide.at[h][pl.ds(base + c, ROWS, stride=COLS), :]
                    colp[stage, side, f * ROWS : (f + 1) * ROWS, h * 128 : h * 128 + 128] = col.astype(BF16)
            for k, (r, c) in enumerate(((0, 0), (0, COLS - 1), (ROWS - 1, 0), (ROWS - 1, COLS - 1))):
                p = base + r * COLS + c
                for h in range(2):
                    cb[stage, k, f : f + 1, h * 128 : h * 128 + 128] = wide[h, p : p + 1]

    sends = []

    def send_halo(stage):
        def send(src, dst, device):
            i = len(copies)
            copy = pltpu.make_async_remote_copy(
                src, dst, ssem.at[stage, i], rsem.at[stage, i], device_id=device, device_id_type=MESH
            )
            copy.start()
            copies.append(copy)

        copies = []
        for g, dt in ((1, 0), (0, 1)):
            for dy, dx, kind, a, b in PIECES:
                device = at(dt, dy, dx)
                if kind == "row":
                    send(buf.at[stage, 2:4, a], buf.at[stage, 2 * g : 2 * g + 2, b], device)
                elif kind == "col":
                    send(colp.at[stage, a], colr.at[stage, g, b], device)
                else:
                    send(cb.at[stage, a], cr.at[stage, g, b], device)
        for f in (1, 0):
            send(
                buf.at[stage, 2 + f, 1 : ROWS + 1], buf.at[stage, f, 1 : ROWS + 1], at(1, 0, 0)
            )
        sends.extend(copies)
        return copies

    def start_a(stage):
        msg[stage, 0] = compact(sums[...])
        for i, (c, k) in enumerate(STEP_A):
            pltpu.make_async_remote_copy(
                msg.at[stage, 0], da.at[stage, i], ssem_a.at[stage], rsem_a.at[stage],
                device_id=on_line(c, k), device_id_type=MESH,
            ).start()

    def end_a_start_b(stage):
        n = len(STEP_A)
        everything = da.at[stage]
        pltpu.make_async_copy(everything, everything, rsem_a.at[stage]).wait()
        total = msg[stage, 0]
        for i in range(n):
            total = total + da[stage, i]
        msg[stage, 1] = total
        for j, k in STEP_B_ORDER:
            pltpu.make_async_remote_copy(
                msg.at[stage, 1], db.at[stage, j * NCHIP + k - 1], ssem_b.at[stage], rsem_b.at[stage],
                device_id=on_plane(j, k), device_id_type=MESH,
            ).start()

    def end_b(stage, gain, shift):
        everything = db.at[stage]
        pltpu.make_async_copy(everything, everything, rsem_b.at[stage]).wait()
        planes = []
        for j in range(NTA):
            total = msg[stage, 1] if j == 0 else db[stage, j * NCHIP - 1]
            for k in range(1, NCHIP):
                total = total + db[stage, j * NCHIP + k - 1]
            planes.append(total if j == 0 else jnp.where(t >= j, total, 0.0))
        red[0] = expand(planes[0])
        red[1] = expand(planes[1])
        red[2] = expand(planes[2] + planes[3])
        running = []
        for s in (0, 4):
            before = red[2, s : s + 2] + red[2, s + 2 : s + 4]
            row = []
            for i in (1, 0):
                for f in range(2):
                    before = before + red[i, s + 2 * f : s + 2 * f + 2]
                    row.append(before)
            running.append(row)
        for f in range(4):
            count = jnp.maximum((2 * t + f - 1).astype(F32), 1.0) * AREA
            mean = running[0][f] / count
            var = running[1][f] / count - mean * mean
            scale = lax.rsqrt(var + EPS) * gain
            sc[0, 2 * f : 2 * f + 2] = scale
            sc[1, 2 * f : 2 * f + 2] = shift - mean * scale

    def silu(a):
        return 0.5 * a * (1.0 + jnp.tanh(0.5 * a))

    def normed(v, f, lanes, h):
        return silu(v * sc[0, f * 2 + h : f * 2 + h + 1] + sc[1, f * 2 + h : f * 2 + h + 1])

    def normalize(stage):
        for g in range(2):
            for f in range(2):
                for h in range(2):
                    lanes = slice(h * 128, h * 128 + 128)
                    for side in range(2):
                        base = ((2 * g + f) * 2 + side) * 32
                        v = colr[stage, g, side, f * ROWS : (f + 1) * ROWS, lanes].astype(F32)
                        hal[h, base + 8 : base + 8 + ROWS] = normed(v, 2 * g + f, lanes, h)
                        for place, k in ((7, side), (8 + ROWS, 2 + side)):
                            v = cr[stage, g, k, f : f + 1, lanes]
                            hal[h, base + place : base + place + 1] = normed(v, 2 * g + f, lanes, h)
        for f in range(4):
            fe = jnp.where(t == 0, 2, f) if f < 2 else f
            rows = [[sc[i, pl.ds(fe * 2 + h, 1)] for h in range(2)] for i in range(2)]

            def step(r, carry):
                re = jnp.where((r == 0) & (gy == 0), 1, r)
                re = jnp.where((r == ROWS + 1) & (gy == NGY - 1), ROWS, re)
                for h in range(2):
                    lanes = slice(h * 128, h * 128 + 128)
                    v = buf[stage, fe, re, :, lanes].astype(F32)
                    n = silu(v * rows[0][h] + rows[1][h])
                    left = hal[h, pl.ds(fe * 64 + 7 + re, 1)]
                    right = hal[h, pl.ds(fe * 64 + 39 + re, 1)]
                    left = jnp.where(gx == 0, n[0:1], left)
                    right = jnp.where(gx == NGX - 1, n[COLS - 1 : COLS], right)
                    xs[1, f, r, :, lanes] = n.astype(BF16)
                    xs[0, f, r, :, lanes] = jnp.where(row_id == 0, left, pltpu.roll(n, 1, 0)).astype(BF16)
                    xs[2, f, r, :, lanes] = jnp.where(
                        row_id == COLS - 1, right, pltpu.roll(n, COLS - 1, 0)
                    ).astype(BF16)
                return carry

            lax.fori_loop(0, ROWS + 2, step, 0, unroll=6)

    def fold_weights():
        def step(u, carry):
            a = u // 4
            p = lax.rem(u // 2, 2)
            d = lax.rem(u, 2)
            both = jnp.where(p != d, 1.0, 0.0).astype(F32)
            main = a * 9 + jnp.where(d == 0, 0, 6)
            zero = jnp.zeros((32, 128), BF16)
            for s in range(0, CH, 32):
                k = [
                    w2[main + c, s : s + 32].astype(F32) + both * w2[a * 9 + 3 + c, s : s + 32].astype(F32)
                    for c in range(3)
                ]
                we[u, 0, s : s + 32, 0:128] = k[0].astype(BF16)
                we[u, 0, s : s + 32, 128:256] = zero
                we[u, 1, s : s + 32, 0:128] = (k[1] + k[2]).astype(BF16)
                we[u, 1, s : s + 32, 128:256] = (k[0] + k[1]).astype(BF16)
                we[u, 2, s : s + 32, 0:128] = zero
                we[u, 2, s : s + 32, 128:256] = k[2].astype(BF16)
            return carry

        lax.fori_loop(0, 12, step, 0)

    load_lat.wait()
    take_in(0, lambda f, r: buf[0, 2 + f, 1 + r].astype(F32))
    pl.semaphore_wait(ready, len(senders))
    start_a(0)
    edges(0)
    halo = send_halo(0)
    for load in loads:
        load.wait()
    fold_weights()
    end_a_start_b(0)
    end_b(0, prm[0], prm[1])
    for copy in halo:
        copy.wait_recv()
    normalize(0)
    total = jnp.zeros((2 * ROWS * COLS, CH), F32)
    for a in range(3):
        for b in range(3):
            for c in range(3):
                piece = xs[c, a : a + 2, b : b + ROWS].reshape(2 * ROWS * COLS, CH)
                total = total + jnp.dot(piece, w1[a * 9 + b * 3 + c], preferred_element_type=F32)
    acc1[...] = total

    bias = jnp.concatenate([prm[2, 0:1], prm[2, 1:2]], axis=1)

    def block_out(f, r):
        conv = acc1[pl.ds(pl.multiple_of((f * ROWS + r) * COLS, COLS), COLS)]
        v = (buf[0, 2 + f, 1 + r].astype(F32) + conv + bias).astype(BF16)
        buf[1, 2 + f, 1 + r] = v
        return v.astype(F32)

    take_in(1, block_out)
    start_a(1)
    edges(1)
    halo = send_halo(1)
    end_a_start_b(1)
    skip[...] = (
        jnp.dot(
            buf[1, 2:4, 1 : ROWS + 1].reshape(2 * ROWS * COLS, CH), ws[...], preferred_element_type=F32
        )
        + b2[...]
    )
    end_b(1, prm[3], prm[4])
    for copy in halo:
        copy.wait_recv()
    normalize(1)
    acc2[...] = jnp.zeros_like(acc2)

    def taps(u, carry):
        a = u // 2
        p = lax.rem(u, 2)
        total = acc2[p]
        for d in range(2):
            for c in range(3):
                piece = xs[c, pl.ds(a, 2), pl.ds(p + d, ROWS)].reshape(2 * ROWS * COLS, CH)
                total = total + jnp.dot(piece, we[u * 2 + d, c], preferred_element_type=F32)
        acc2[p] = total
        return carry

    lax.fori_loop(0, 6, taps, 0)

    def finish(u, carry):
        f = u // ROWS
        i = lax.rem(u, ROWS)
        place = pl.ds(pl.multiple_of(u * COLS, COLS), COLS)
        extra = skip[place]
        for p in range(2):
            for q in range(2):
                v = acc2[p, place, q * CO : (q + 1) * CO] + extra
                tmp[lax.rem(u, 2) * 2 + p, pl.ds(q, COLS, stride=2), :] = v
            ob[f, i * 2 + p] = tmp[lax.rem(u, 2) * 2 + p].astype(BF16)
        return carry

    for f in range(2):
        lax.fori_loop(f * ROWS, (f + 1) * ROWS, finish, 0, unroll=4)
        pltpu.make_async_copy(ob.at[f], out.at[f], osem.at[f]).start()

    for copy in sends:
        copy.wait_send()
    for stage in range(2):
        pltpu.make_async_copy(da.at[stage], da.at[stage], ssem_a.at[stage]).wait()
        pltpu.make_async_copy(db.at[stage], db.at[stage], ssem_b.at[stage]).wait()
    for f in range(2):
        pltpu.make_async_copy(ob.at[f], out.at[f], osem.at[f]).wait()


def on_device(
    latents, gain_one, shift_one, weight_one, bias_one, gain_two, shift_two, weight_two, weight_skip, bias_two
):
    vmem = pltpu.VMEM
    dma = pltpu.SemaphoreType.DMA
    n_halo = 2 * len(PIECES) + 2
    halves = lambda v: v.reshape(2, 128)
    return pl.pallas_call(
        kernel,
        out_shape=jax.ShapeDtypeStruct((2, 2 * ROWS, 2 * COLS, CO), BF16),
        in_specs=[pl.BlockSpec(memory_space=pl.ANY)] * 10,
        out_specs=pl.BlockSpec(memory_space=pl.ANY),
        scratch_shapes=[
            vmem((2, 4, ROWS + 2, COLS, CH), BF16),
            vmem((2, 2, 2 * ROWS, CH), BF16),
            vmem((2, 2, 2, 2 * ROWS, CH), BF16),
            vmem((2, 4, 2, CH), F32),
            vmem((2, 2, 4, 2, CH), F32),
            vmem((2, 2 * ROWS * COLS, 128), F32),
            vmem((3, 4, ROWS + 2, COLS, CH), BF16),
            vmem((2, 8 * 32, 128), F32),
            vmem((8, 128), F32),
            vmem((3, 8, 128), F32),
            vmem((2, 8, 128), F32),
            vmem((27, CH, CH), BF16),
            vmem((27, CH, CO), BF16),
            vmem((12, 3, CH, 2 * CO), BF16),
            vmem((CH, CO), BF16),
            vmem((5, 2, 128), F32),
            vmem((1, CO), F32),
            vmem((2 * ROWS * COLS, CH), F32),
            vmem((2, 2 * ROWS * COLS, 2 * CO), F32),
            vmem((2 * ROWS * COLS, CO), F32),
            vmem((4, 2 * COLS, CO), F32),
            vmem((2, 2 * ROWS, 2 * COLS, CO), BF16),
            vmem((2, 2, 1, 128), F32),
            vmem((2, len(STEP_A), 1, 128), F32),
            vmem((2, len(STEP_B), 1, 128), F32),
            dma((2, n_halo)),
            dma((2, n_halo)),
            dma((2,)),
            dma((2,)),
            dma((2,)),
            dma((2,)),
            dma((10,)),
            dma((2,)),
        ],
        compiler_params=pltpu.CompilerParams(
            collective_id=0, has_side_effects=True, vmem_limit_bytes=52 << 20
        ),
    )(
        latents,
        weight_one.reshape(27, CH, CH),
        weight_two.reshape(27, CH, CO),
        weight_skip,
        halves(gain_one),
        halves(shift_one),
        halves(bias_one),
        halves(gain_two),
        halves(shift_two),
        bias_two.reshape(1, CO),
    )


def solution(mesh):
    in_specs = (P("ta", "gy", "gx", None),) + (P(),) * 9
    return jax.shard_map(
        on_device, mesh=mesh, in_specs=in_specs, out_specs=P("ta", "gy", "gx", None), check_vma=False
    )
```

time: 383 us -> 47.6 us (0.12)
  blocking collectives: 257 us -> 0 us
  Pallas kernels: 0 us -> 40.7 us
  starting transfers between devices: 40.5 us -> 0 us
  other arithmetic: 27.7 us -> 0 us
  waiting for transfers between devices: 25.8 us -> 0 us
  matrix products: 19.1 us -> 0 us
  local copies, waits for them, and re-layouts: 11.3 us -> 6.63 us
    psum x2 -> x0, blocking collectives: 241 us -> none  [cumulative(): grid = lax.psum(local, ('gy', 'gx'))]
    pallas_call x0 -> x1, Pallas kernels: none -> 40.7 us  [on_device(): pl.pallas_call(kernel, out_shape=jax.ShapeDtypeStruct((2, 2 * ROWS, 2 * C...]
    ppermute x10 -> x0, starting transfers between devices: 40.5 us -> none  [the longest x4 28 us: padded_2(): lax.ppermute(lax.slice_in_dim(block, 0, width, axis=dim), axis, backward)]
    ppermute x10 -> x0, waiting for transfers between devices: 25.8 us -> none  [the longest x2 15.2 us: shifted(): lax.ppermute(value, axis, [(source, source + steps) for source in range(l...]
    concatenate x12 -> x0, other arithmetic: 20.7 us -> none  [the longest x4 13.8 us: edge_fix(): return jnp.concatenate([left, padded[:, :, 1:-1], right], axis=2)]
    dot_general x55 -> x0, matrix products: 19.1 us -> none  [the longest x54 17.8 us: convolve(): jnp.dot(piece, kernel[a, b, c], preferred_element_type=jnp.float32)]
    all_gather x2 -> x0, blocking collectives: 15.8 us -> none  [prefix_2(): everything = lax.all_gather(array, axis)]
    unnamed x16 -> x17, local copies, waits for them, and re-layouts: 1.05 us -> 6.63 us
  transfers between devices with their start and end apart: 10 -> 0, of which waited for: 7 -> 0; matrix products, arithmetic and copies ran while one was open for 1% -> 0% of each run, Pallas kernels for 0% -> 0%
where the time goes in v1:
time: 47.6 us; the launch traced here: 47.4 us
  Pallas kernels  40.7 us (86%)
  local copies, waits for them, and re-layouts  6.63 us (14%)
    pallas_call x1, Pallas kernels, on_device(): pl.pallas_call(kernel, out_shape=jax.ShapeDtypeStruct((2, 2 * ROWS, 2 * C...  40.7 us
    unnamed x17, local copies, waits for them, and re-layouts  6.63 us

profile of v1, /device:TPU:1, one launch (start us, length us, event | category | flops | bytes accessed | tf_op | source)
XLA Modules:
  0.0 47.4 jit_solution(3940613699612369467)
XLA Ops:
  0.0 0.0 copy-start
  0.0 0.9 %copy-done = bf16[2,16,16,256]{3,2,1,0:T(8,128)(2,1)S(1)} copy-done((bf16[2,16,16,256]{3,2,1,0:T(8,128)(2,1)S(1)}, bf16[2,16,16,256]{3,2,1,0:T(8,128)(2,1)}, u32[]{:S(2)}) %copy-start) | copy-done | bytes 262168
  1.0 0.0 copy-start.1
  1.0 0.8 %copy-done.1 = bf16[256,128]{1,0:T(8,128)(2,1)S(1)} copy-done((bf16[256,128]{1,0:T(8,128)(2,1)S(1)}, bf16[256,128]{1,0:T(8,128)(2,1)}, u32[]{:S(2)}) %copy-start.1) | copy-done | bytes 65560
  1.8 0.0 copy-start.2
  1.8 0.7 %copy-done.2 = f32[256]{0:T(256)S(1)} copy-done((f32[256]{0:T(256)S(1)}, f32[256]{0:T(256)}, u32[]{:S(2)}) %copy-start.2) | copy-done | bytes 1048
  2.5 0.0 copy-start.3
  2.5 0.7 %copy-done.3 = f32[256]{0:T(256)S(1)} copy-done((f32[256]{0:T(256)S(1)}, f32[256]{0:T(256)}, u32[]{:S(2)}) %copy-start.3) | copy-done | bytes 1048
  3.1 0.0 copy-start.4
  3.2 0.7 %copy-done.4 = f32[256]{0:T(256)S(1)} copy-done((f32[256]{0:T(256)S(1)}, f32[256]{0:T(256)}, u32[]{:S(2)}) %copy-start.4) | copy-done | bytes 1048
  3.8 0.0 copy-start.5
  3.8 0.7 %copy-done.5 = f32[256]{0:T(256)S(1)} copy-done((f32[256]{0:T(256)S(1)}, f32[256]{0:T(256)}, u32[]{:S(2)}) %copy-start.5) | copy-done | bytes 1048
  4.5 0.0 copy-start.6
  4.5 0.7 %copy-done.6 = f32[256]{0:T(256)S(1)} copy-done((f32[256]{0:T(256)S(1)}, f32[256]{0:T(256)}, u32[]{:S(2)}) %copy-start.6) | copy-done | bytes 1048
  5.2 0.0 copy-start.7
  5.2 0.7 %copy-done.7 = f32[128]{0:T(128)S(1)} copy-done((f32[128]{0:T(128)S(1)}, f32[128]{0:T(128)}, u32[]{:S(2)}) %copy-start.7) | copy-done | bytes 536
  5.8 40.7 %shard_map.100 = bf16[2,32,32,128]{3,2,1,0:T(8,128)(2,1)S(1)} custom-call(bf16[2,16,16,256]{3,2,1,0:T(8,128)(2,1)S(1)} %copy-done, bf16[27,256,256]{2,1,0:T(8,128)(2,1)} %bitcast.14, bf16[27,256,128]{2,1,0:T(8,128)(2,1)} %bitcast.15, bf16[256,128]{1,0:T(8,128)(2,1)S(1)} %copy-done.1, f32[2,128]{1,0:T(2,128)S(1)} %bitcast.8, f32[2,128]{1,0:T(2,128)S(1)} %bitcast.9, ...), custom_call_target="tpu_custom_call" | custom-call | tf_op jit(solution)/shard_map/pallas_call | solution.py:359
  46.6 0.8 %copy.12 = bf16[2,32,32,128]{3,2,1,0:T(8,128)(2,1)} copy(bf16[2,32,32,128]{3,2,1,0:T(8,128)(2,1)S(1)} %shard_map.100) | data formatting | bytes 1048576
Async XLA Ops:
  0.0 0.9 %copy-start = (bf16[2,16,16,256]{3,2,1,0:T(8,128)(2,1)S(1)}, bf16[2,16,16,256]{3,2,1,0:T(8,128)(2,1)}, u32[]{:S(2)}) copy-start(bf16[2,16,16,256]{3,2,1,0:T(8,128)(2,1)} %lat.1) | copy-start | bytes 786436
  1.0 0.8 %copy-start.1 = (bf16[256,128]{1,0:T(8,128)(2,1)S(1)}, bf16[256,128]{1,0:T(8,128)(2,1)}, u32[]{:S(2)}) copy-start(bf16[256,128]{1,0:T(8,128)(2,1)} %wsh.1) | copy-start | bytes 196612
  1.8 0.7 %copy-start.2 = (f32[256]{0:T(256)S(1)}, f32[256]{0:T(256)}, u32[]{:S(2)}) copy-start(f32[256]{0:T(256)} %param.11) | copy-start | bytes 3076
  2.5 0.7 %copy-start.3 = (f32[256]{0:T(256)S(1)}, f32[256]{0:T(256)}, u32[]{:S(2)}) copy-start(f32[256]{0:T(256)} %param.12) | copy-start | bytes 3076
  3.1 0.7 %copy-start.4 = (f32[256]{0:T(256)S(1)}, f32[256]{0:T(256)}, u32[]{:S(2)}) copy-start(f32[256]{0:T(256)} %param.14) | copy-start | bytes 3076
  3.8 0.7 %copy-start.5 = (f32[256]{0:T(256)S(1)}, f32[256]{0:T(256)}, u32[]{:S(2)}) copy-start(f32[256]{0:T(256)} %param.15) | copy-start | bytes 3076
  4.5 0.7 %copy-start.6 = (f32[256]{0:T(256)S(1)}, f32[256]{0:T(256)}, u32[]{:S(2)}) copy-start(f32[256]{0:T(256)} %param.16) | copy-start | bytes 3076
  5.2 0.7 %copy-start.7 = (f32[128]{0:T(128)S(1)}, f32[128]{0:T(128)}, u32[]{:S(2)}) copy-start(f32[128]{0:T(128)} %param.19) | copy-start | bytes 1540

commit v2 on v1

--- a/solution.py
+++ b/solution.py
@@ -15,9 +15,9 @@
 ROWS, COLS, CH, CO = 16, 16, 256, 128
 AREA = float(NGY * ROWS * NGX * COLS * (CH // 32))
 
-STEP_A = [(c, k) for k in (4, 3, -3, 2, -2, 1, -1, 0) for c in (1, 0) if (c, k) != (0, 0)]
-STEP_B = [(j, k) for j in range(NTA) for k in range(NCHIP) if (j, k) != (0, 0)]
-STEP_B_ORDER = sorted(STEP_B, key=lambda p: -(min(p[0], NTA - p[0]) + min(p[1], NCHIP - p[1])))
+PLANE = [(j, k) for j in range(NTA) for k in range(NCHIP) if (j, k) != (0, 0)]
+PLANE_FAR_FIRST = sorted(PLANE, key=lambda p: -(min(p[0], NTA - p[0]) + min(p[1], NCHIP - p[1])))
+LINE = [(c, k) for k in (4, 3, -3, 2, -2, 1, -1, 0) for c in (1, 0) if (c, k) != (0, 0)]
 
 PIECES = [
     (-1, 0, "row", 1, ROWS + 1),
@@ -37,9 +37,9 @@
 
 def kernel(
     lat, w1h, w2h, wsh, g1h, s1h, b1h, g2h, s2h, b2h, out,
-    buf, colp, colr, cb, cr, wide, xs, hal, sums, red, sc, w1, w2, we, ws, prm, b2,
-    acc1, acc2, skip, tmp, ob,
-    msg, da, db, ssem, rsem, ssem_a, rsem_a, ssem_b, rsem_b, lsem, osem,
+    buf, colp, colr, cb, cr, wide, xs, hal, sums, red, sc, w1, w2, wc, we, wg, ws, prm, b2,
+    acc1, acc2, acce, accg, skip, tmp, ob,
+    msg, msg3, da, db, ssem, rsem, ssem_a, rsem_a, ssem_b, rsem_b, lsem, osem,
 ):
     t = lax.axis_index("ta")
     gy = lax.axis_index("gy")
@@ -56,7 +56,7 @@
         return (wrap(t + j, NTA), wrap(chip + k, NCHIP) * 2 + core, gx)
 
     ready = pltpu.get_barrier_semaphore()
-    senders = [on_line(c, k) for c, k in STEP_A] + [on_plane(j, k) for j, k in STEP_B]
+    senders = [on_plane(j, k) for j, k in PLANE_FAR_FIRST] + [on_line(c, k) for c, k in LINE]
     senders += [at(0, dy, dx) for dy, dx, _, _, _ in PIECES]
     senders += [at(-1, 0, 0)] + [at(-1, dy, dx) for dy, dx, _, _, _ in PIECES]
     load_lat = pltpu.make_async_copy(lat, buf.at[0, 2:4, 1 : ROWS + 1], lsem.at[0])
@@ -141,47 +141,45 @@
                     send(colp.at[stage, a], colr.at[stage, g, b], device)
                 else:
                     send(cb.at[stage, a], cr.at[stage, g, b], device)
-        for f in (1, 0):
-            send(
-                buf.at[stage, 2 + f, 1 : ROWS + 1], buf.at[stage, f, 1 : ROWS + 1], at(1, 0, 0)
-            )
+            if g == 1:
+                for f in (1, 0):
+                    send(buf.at[stage, 2 + f, 1 : ROWS + 1], buf.at[stage, f, 1 : ROWS + 1], at(1, 0, 0))
         sends.extend(copies)
-        return copies
-
-    def start_a(stage):
-        msg[stage, 0] = compact(sums[...])
-        for i, (c, k) in enumerate(STEP_A):
+        near = len(PIECES)
+        return copies[:near], copies[near:]
+
+    def start_plane(stage):
+        msg[stage] = compact(sums[...])
+        for j, k in PLANE_FAR_FIRST:
             pltpu.make_async_remote_copy(
-                msg.at[stage, 0], da.at[stage, i], ssem_a.at[stage], rsem_a.at[stage],
+                msg.at[stage], da.at[stage, j * NCHIP + k - 1], ssem_a.at[stage], rsem_a.at[stage],
+                device_id=on_plane(j, k), device_id_type=MESH,
+            ).start()
+
+    def start_line(stage):
+        everything = da.at[stage]
+        pltpu.make_async_copy(everything, everything, rsem_a.at[stage]).wait()
+        spans = []
+        for j in range(NTA):
+            total = msg[stage] if j == 0 else da[stage, j * NCHIP - 1]
+            for k in range(1, NCHIP):
+                total = total + da[stage, j * NCHIP + k - 1]
+            spans.append(total if j == 0 else jnp.where(t >= j, total, 0.0))
+        msg3[stage] = jnp.concatenate([spans[0], spans[1], spans[2] + spans[3]], axis=1)
+        for i, (c, k) in enumerate(LINE):
+            pltpu.make_async_remote_copy(
+                msg3.at[stage], db.at[stage, i], ssem_b.at[stage], rsem_b.at[stage],
                 device_id=on_line(c, k), device_id_type=MESH,
             ).start()
 
-    def end_a_start_b(stage):
-        n = len(STEP_A)
-        everything = da.at[stage]
-        pltpu.make_async_copy(everything, everything, rsem_a.at[stage]).wait()
-        total = msg[stage, 0]
-        for i in range(n):
-            total = total + da[stage, i]
-        msg[stage, 1] = total
-        for j, k in STEP_B_ORDER:
-            pltpu.make_async_remote_copy(
-                msg.at[stage, 1], db.at[stage, j * NCHIP + k - 1], ssem_b.at[stage], rsem_b.at[stage],
-                device_id=on_plane(j, k), device_id_type=MESH,
-            ).start()
-
-    def end_b(stage, gain, shift):
+    def end_line(stage, gain, shift):
         everything = db.at[stage]
         pltpu.make_async_copy(everything, everything, rsem_b.at[stage]).wait()
-        planes = []
-        for j in range(NTA):
-            total = msg[stage, 1] if j == 0 else db[stage, j * NCHIP - 1]
-            for k in range(1, NCHIP):
-                total = total + db[stage, j * NCHIP + k - 1]
-            planes.append(total if j == 0 else jnp.where(t >= j, total, 0.0))
-        red[0] = expand(planes[0])
-        red[1] = expand(planes[1])
-        red[2] = expand(planes[2] + planes[3])
+        total = msg3[stage]
+        for i in range(len(LINE)):
+            total = total + db[stage, i]
+        for i in range(3):
+            red[i] = expand(total[:, i * 128 : i * 128 + 128])
         running = []
         for s in (0, 4):
             before = red[2, s : s + 2] + red[2, s + 2 : s + 4]
@@ -202,23 +200,23 @@
     def silu(a):
         return 0.5 * a * (1.0 + jnp.tanh(0.5 * a))
 
-    def normed(v, f, lanes, h):
-        return silu(v * sc[0, f * 2 + h : f * 2 + h + 1] + sc[1, f * 2 + h : f * 2 + h + 1])
-
-    def normalize(stage):
-        for g in range(2):
-            for f in range(2):
-                for h in range(2):
-                    lanes = slice(h * 128, h * 128 + 128)
-                    for side in range(2):
-                        base = ((2 * g + f) * 2 + side) * 32
-                        v = colr[stage, g, side, f * ROWS : (f + 1) * ROWS, lanes].astype(F32)
-                        hal[h, base + 8 : base + 8 + ROWS] = normed(v, 2 * g + f, lanes, h)
-                        for place, k in ((7, side), (8 + ROWS, 2 + side)):
-                            v = cr[stage, g, k, f : f + 1, lanes]
-                            hal[h, base + place : base + place + 1] = normed(v, 2 * g + f, lanes, h)
-        for f in range(4):
-            fe = jnp.where(t == 0, 2, f) if f < 2 else f
+    def normalize(stage, g):
+        for f in range(2):
+            for h in range(2):
+                lanes = slice(h * 128, h * 128 + 128)
+                frame = 2 * g + f
+                scale, shift = sc[0, pl.ds(frame * 2 + h, 1)], sc[1, pl.ds(frame * 2 + h, 1)]
+                for side in range(2):
+                    base = pl.multiple_of((frame * 2 + side) * 32, 32)
+                    v = colr[stage, g, side, f * ROWS : (f + 1) * ROWS, lanes].astype(F32)
+                    hal[h, pl.ds(base + 8, ROWS)] = silu(v * scale + shift)
+                    for place, k in ((7, side), (8 + ROWS, 2 + side)):
+                        v = cr[stage, g, k, f : f + 1, lanes]
+                        hal[h, pl.ds(base + place, 1)] = silu(v * scale + shift)
+
+        def frame_step(f, carry):
+            frame = 2 * g + f
+            fe = jnp.where((t == 0) & (frame < 2), 2, frame)
             rows = [[sc[i, pl.ds(fe * 2 + h, 1)] for h in range(2)] for i in range(2)]
 
             def step(r, carry):
@@ -232,59 +230,93 @@
                     right = hal[h, pl.ds(fe * 64 + 39 + re, 1)]
                     left = jnp.where(gx == 0, n[0:1], left)
                     right = jnp.where(gx == NGX - 1, n[COLS - 1 : COLS], right)
-                    xs[1, f, r, :, lanes] = n.astype(BF16)
-                    xs[0, f, r, :, lanes] = jnp.where(row_id == 0, left, pltpu.roll(n, 1, 0)).astype(BF16)
-                    xs[2, f, r, :, lanes] = jnp.where(
+                    xs[1, frame, r, :, lanes] = n.astype(BF16)
+                    xs[0, frame, r, :, lanes] = jnp.where(row_id == 0, left, pltpu.roll(n, 1, 0)).astype(BF16)
+                    xs[2, frame, r, :, lanes] = jnp.where(
                         row_id == COLS - 1, right, pltpu.roll(n, COLS - 1, 0)
                     ).astype(BF16)
                 return carry
 
-            lax.fori_loop(0, ROWS + 2, step, 0, unroll=6)
+            return lax.fori_loop(0, ROWS + 2, step, carry, unroll=6)
+
+        lax.fori_loop(0, 2, frame_step, 0)
 
     def fold_weights():
         def step(u, carry):
-            a = u // 4
-            p = lax.rem(u // 2, 2)
-            d = lax.rem(u, 2)
-            both = jnp.where(p != d, 1.0, 0.0).astype(F32)
-            main = a * 9 + jnp.where(d == 0, 0, 6)
-            zero = jnp.zeros((32, 128), BF16)
-            for s in range(0, CH, 32):
-                k = [
-                    w2[main + c, s : s + 32].astype(F32) + both * w2[a * 9 + 3 + c, s : s + 32].astype(F32)
-                    for c in range(3)
-                ]
-                we[u, 0, s : s + 32, 0:128] = k[0].astype(BF16)
-                we[u, 0, s : s + 32, 128:256] = zero
-                we[u, 1, s : s + 32, 0:128] = (k[1] + k[2]).astype(BF16)
-                we[u, 1, s : s + 32, 128:256] = (k[0] + k[1]).astype(BF16)
-                we[u, 2, s : s + 32, 0:128] = zero
-                we[u, 2, s : s + 32, 128:256] = k[2].astype(BF16)
+            a = u // 8
+            rows = pl.ds(pl.multiple_of(lax.rem(u, 8) * 32, 32), 32)
+            k = [[w2[a * 9 + b * 3 + c, rows].astype(F32) for c in range(3)] for b in range(3)]
+            upper = [k[1][c] + k[2][c] for c in range(3)]
+            lower = [k[0][c] + k[1][c] for c in range(3)]
+            for i, v in enumerate((k[0], upper, lower, k[2])):
+                wc[a * 4 + i, rows, 0:CO] = (v[1] + v[2]).astype(BF16)
+                wc[a * 4 + i, rows, CO : 2 * CO] = (v[0] + v[1]).astype(BF16)
+            for q in range(2):
+                we[a * 2 + q, rows, 0:CO] = upper[2 * q].astype(BF16)
+                we[a * 2 + q, rows, CO : 2 * CO] = lower[2 * q].astype(BF16)
+                wg[a * 2 + q, rows, 0:CO] = k[0][2 * q].astype(BF16)
+                wg[a * 2 + q, rows, CO : 2 * CO] = k[2][2 * q].astype(BF16)
             return carry
 
-        lax.fori_loop(0, 12, step, 0)
+        lax.fori_loop(0, 24, step, 0)
+
+    def dot(x, w):
+        return jnp.dot(x, w, preferred_element_type=F32)
+
+    def flat(piece):
+        return piece.reshape(-1, CH)
+
+    def conv_one(a):
+        total = acc1[...]
+        for b in range(3):
+            for c in range(3):
+                total = total + dot(flat(xs[c, pl.ds(a, 2), b : b + ROWS]), w1[a * 9 + b * 3 + c])
+        acc1[...] = total
+
+    def conv_two(a):
+        for p in range(2):
+            total = acc2[p]
+            for d in range(2):
+                total = total + dot(flat(xs[1, pl.ds(a, 2), p + d : p + d + ROWS]), wc[a * 4 + p * 2 + d])
+            acc2[p] = total
+        for q in range(2):
+            acce[q] += dot(flat(xs[2 * q, pl.ds(a, 2), 1 : 1 + ROWS]), we[a * 2 + q])
+            accg[q] += dot(flat(xs[2 * q, pl.ds(a, 2)]), wg[a * 2 + q])
+
+    def norm_and_convolve(stage, conv, near, far):
+        def step(i, carry):
+            @pl.when(i == 0)
+            def _():
+                for copy in near:
+                    copy.wait_recv()
+
+            @pl.when(i == 1)
+            def _():
+                for copy in far:
+                    copy.wait_recv()
+
+            @pl.when(i < 2)
+            def _():
+                normalize(stage, 1 - i)
+
+            conv(2 - i)
+            return carry
+
+        lax.fori_loop(0, 3, step, 0)
 
     load_lat.wait()
     take_in(0, lambda f, r: buf[0, 2 + f, 1 + r].astype(F32))
     pl.semaphore_wait(ready, len(senders))
-    start_a(0)
+    start_plane(0)
     edges(0)
-    halo = send_halo(0)
+    near, far = send_halo(0)
     for load in loads:
         load.wait()
+    start_line(0)
     fold_weights()
-    end_a_start_b(0)
-    end_b(0, prm[0], prm[1])
-    for copy in halo:
-        copy.wait_recv()
-    normalize(0)
-    total = jnp.zeros((2 * ROWS * COLS, CH), F32)
-    for a in range(3):
-        for b in range(3):
-            for c in range(3):
-                piece = xs[c, a : a + 2, b : b + ROWS].reshape(2 * ROWS * COLS, CH)
-                total = total + jnp.dot(piece, w1[a * 9 + b * 3 + c], preferred_element_type=F32)
-    acc1[...] = total
+    acc1[...] = jnp.zeros_like(acc1)
+    end_line(0, prm[0], prm[1])
+    norm_and_convolve(0, conv_one, near, far)
 
     bias = jnp.concatenate([prm[2, 0:1], prm[2, 1:2]], axis=1)
 
@@ -295,34 +327,16 @@
         return v.astype(F32)
 
     take_in(1, block_out)
-    start_a(1)
+    start_plane(1)
     edges(1)
-    halo = send_halo(1)
-    end_a_start_b(1)
-    skip[...] = (
-        jnp.dot(
-            buf[1, 2:4, 1 : ROWS + 1].reshape(2 * ROWS * COLS, CH), ws[...], preferred_element_type=F32
-        )
-        + b2[...]
-    )
-    end_b(1, prm[3], prm[4])
-    for copy in halo:
-        copy.wait_recv()
-    normalize(1)
+    near, far = send_halo(1)
+    skip[...] = dot(buf[1, 2:4, 1 : ROWS + 1].reshape(2 * ROWS * COLS, CH), ws[...]) + b2[...]
+    start_line(1)
     acc2[...] = jnp.zeros_like(acc2)
-
-    def taps(u, carry):
-        a = u // 2
-        p = lax.rem(u, 2)
-        total = acc2[p]
-        for d in range(2):
-            for c in range(3):
-                piece = xs[c, pl.ds(a, 2), pl.ds(p + d, ROWS)].reshape(2 * ROWS * COLS, CH)
-                total = total + jnp.dot(piece, we[u * 2 + d, c], preferred_element_type=F32)
-        acc2[p] = total
-        return carry
-
-    lax.fori_loop(0, 6, taps, 0)
+    acce[...] = jnp.zeros_like(acce)
+    accg[...] = jnp.zeros_like(accg)
+    end_line(1, prm[3], prm[4])
+    norm_and_convolve(1, conv_two, near, far)
 
     def finish(u, carry):
         f = u // ROWS
@@ -331,7 +345,9 @@
         extra = skip[place]
         for p in range(2):
             for q in range(2):
-                v = acc2[p, place, q * CO : (q + 1) * CO] + extra
+                outer = pl.ds(pl.multiple_of((u + 2 * f + 2 * p) * COLS, COLS), COLS)
+                v = acc2[p, place, q * CO : (q + 1) * CO] + acce[q, place, p * CO : (p + 1) * CO]
+                v = v + (accg[q, outer, p * CO : (p + 1) * CO] + extra)
                 tmp[lax.rem(u, 2) * 2 + p, pl.ds(q, COLS, stride=2), :] = v
             ob[f, i * 2 + p] = tmp[lax.rem(u, 2) * 2 + p].astype(BF16)
         return carry
@@ -375,18 +391,23 @@
             vmem((2, 8, 128), F32),
             vmem((27, CH, CH), BF16),
             vmem((27, CH, CO), BF16),
-            vmem((12, 3, CH, 2 * CO), BF16),
+            vmem((12, CH, 2 * CO), BF16),
+            vmem((6, CH, 2 * CO), BF16),
+            vmem((6, CH, 2 * CO), BF16),
             vmem((CH, CO), BF16),
             vmem((5, 2, 128), F32),
             vmem((1, CO), F32),
             vmem((2 * ROWS * COLS, CH), F32),
             vmem((2, 2 * ROWS * COLS, 2 * CO), F32),
+            vmem((2, 2 * ROWS * COLS, 2 * CO), F32),
+            vmem((2, 2 * (ROWS + 2) * COLS, 2 * CO), F32),
             vmem((2 * ROWS * COLS, CO), F32),
             vmem((4, 2 * COLS, CO), F32),
             vmem((2, 2 * ROWS, 2 * COLS, CO), BF16),
-            vmem((2, 2, 1, 128), F32),
-            vmem((2, len(STEP_A), 1, 128), F32),
-            vmem((2, len(STEP_B), 1, 128), F32),
+            vmem((2, 1, 128), F32),
+            vmem((2, 1, 384), F32),
+            vmem((2, len(PLANE), 1, 128), F32),
+            vmem((2, len(LINE), 1, 384), F32),
             dma((2, n_halo)),
             dma((2, n_halo)),
             dma((2,)),
@@ -397,7 +418,7 @@
             dma((2,)),
         ],
         compiler_params=pltpu.CompilerParams(
-            collective_id=0, has_side_effects=True, vmem_limit_bytes=52 << 20
+            collective_id=0, has_side_effects=True, vmem_limit_bytes=62 << 20
         ),
     )(
         latents,

time: 47.6 us -> 40.3 us (0.85)
  local copies, waits for them, and re-layouts: 6.63 us -> 1.87 us
  Pallas kernels: 40.7 us -> 38.3 us
    unnamed x17 -> x1, local copies, waits for them, and re-layouts: 6.63 us -> 1.87 us
    pallas_call x1, Pallas kernels: 40.7 us -> 38.3 us  [on_device(): pl.pallas_call(kernel, out_shape=jax.ShapeDtypeStruct((2, 2 * ROWS, 2 * C...]
where the time goes in v2:
time: 40.3 us; the launch traced here: 40.2 us
  Pallas kernels  38.3 us (95%)
  local copies, waits for them, and re-layouts  1.87 us (5%)
    pallas_call x1, Pallas kernels, on_device(): pl.pallas_call(kernel, out_shape=jax.ShapeDtypeStruct((2, 2 * ROWS, 2 * C...  38.3 us
    unnamed x1, local copies, waits for them, and re-layouts  1.87 us

profile of v2, /device:TPU:1, one launch (start us, length us, event | category | flops | bytes accessed | tf_op | source)
XLA Modules:
  0.0 40.2 jit_solution(12474189589502900604)
XLA Ops:
  0.0 38.3 %shard_map.100 = bf16[2,32,32,128]{3,2,1,0:T(8,128)(2,1)} custom-call(bf16[2,16,16,256]{3,2,1,0:T(8,128)(2,1)} %lat.1, bf16[27,256,256]{2,1,0:T(8,128)(2,1)} %bitcast.8, bf16[27,256,128]{2,1,0:T(8,128)(2,1)} %bitcast.9, bf16[256,128]{1,0:T(8,128)(2,1)} %wsh.1, f32[2,128]{1,0:T(2,128)} %bitcast.10, f32[2,128]{1,0:T(2,128)} %bitcast.11, f32[2,128]{1,0:T(2,128)} %bitcast.12, ...), custom_call_target="tpu_custom_call" | custom-call | tf_op jit(solution)/shard_map/pallas_call | solution.py:375
  38.3 1.9 %copy.12 = bf16[2,32,32,128]{3,2,1,0:T(8,128)(2,1)} copy(bf16[2,32,32,128]{3,2,1,0:T(8,128)(2,1)} %shard_map.100) | data formatting | bytes 1048576

commit v3 on v2

--- a/solution.py
+++ b/solution.py
@@ -1,3 +1,5 @@
+import functools
+
 import jax
 import jax.numpy as jnp
 from jax import lax
@@ -38,7 +40,7 @@
 def kernel(
     lat, w1h, w2h, wsh, g1h, s1h, b1h, g2h, s2h, b2h, out,
     buf, colp, colr, cb, cr, wide, xs, hal, sums, red, sc, w1, w2, wc, we, wg, ws, prm, b2,
-    acc1, acc2, acce, accg, skip, tmp, ob,
+    acc1, acc2, acce, accg, tmp, ob,
     msg, msg3, da, db, ssem, rsem, ssem_a, rsem_a, ssem_b, rsem_b, lsem, osem,
 ):
     t = lax.axis_index("ta")
@@ -200,7 +202,7 @@
     def silu(a):
         return 0.5 * a * (1.0 + jnp.tanh(0.5 * a))
 
-    def normalize(stage, g):
+    def norm_edges(stage, g):
         for f in range(2):
             for h in range(2):
                 lanes = slice(h * 128, h * 128 + 128)
@@ -214,27 +216,37 @@
                         v = cr[stage, g, k, f : f + 1, lanes]
                         hal[h, pl.ds(base + place, 1)] = silu(v * scale + shift)
 
+    def norm_rows(stage, frame):
+        fe = jnp.where((t == 0) & (frame < 2), 2, frame)
+        rows = [[sc[i, pl.ds(fe * 2 + h, 1)] for h in range(2)] for i in range(2)]
+
+        def step(r):
+            re = jnp.where((r == 0) & (gy == 0), 1, r)
+            re = jnp.where((r == ROWS + 1) & (gy == NGY - 1), ROWS, re)
+            for h in range(2):
+                lanes = slice(h * 128, h * 128 + 128)
+                v = buf[stage, fe, re, :, lanes].astype(F32)
+                n = silu(v * rows[0][h] + rows[1][h])
+                left = hal[h, pl.ds(fe * 64 + 7 + re, 1)]
+                right = hal[h, pl.ds(fe * 64 + 39 + re, 1)]
+                left = jnp.where(gx == 0, n[0:1], left)
+                right = jnp.where(gx == NGX - 1, n[COLS - 1 : COLS], right)
+                xs[1, frame, r, :, lanes] = n.astype(BF16)
+                xs[0, frame, r, :, lanes] = jnp.where(row_id == 0, left, pltpu.roll(n, 1, 0)).astype(BF16)
+                xs[2, frame, r, :, lanes] = jnp.where(
+                    row_id == COLS - 1, right, pltpu.roll(n, COLS - 1, 0)
+                ).astype(BF16)
+
+        return step
+
+    def normalize(stage, g):
+        norm_edges(stage, g)
+
         def frame_step(f, carry):
-            frame = 2 * g + f
-            fe = jnp.where((t == 0) & (frame < 2), 2, frame)
-            rows = [[sc[i, pl.ds(fe * 2 + h, 1)] for h in range(2)] for i in range(2)]
+            row_step = norm_rows(stage, 2 * g + f)
 
             def step(r, carry):
-                re = jnp.where((r == 0) & (gy == 0), 1, r)
-                re = jnp.where((r == ROWS + 1) & (gy == NGY - 1), ROWS, re)
-                for h in range(2):
-                    lanes = slice(h * 128, h * 128 + 128)
-                    v = buf[stage, fe, re, :, lanes].astype(F32)
-                    n = silu(v * rows[0][h] + rows[1][h])
-                    left = hal[h, pl.ds(fe * 64 + 7 + re, 1)]
-                    right = hal[h, pl.ds(fe * 64 + 39 + re, 1)]
-                    left = jnp.where(gx == 0, n[0:1], left)
-                    right = jnp.where(gx == NGX - 1, n[COLS - 1 : COLS], right)
-                    xs[1, frame, r, :, lanes] = n.astype(BF16)
-                    xs[0, frame, r, :, lanes] = jnp.where(row_id == 0, left, pltpu.roll(n, 1, 0)).astype(BF16)
-                    xs[2, frame, r, :, lanes] = jnp.where(
-                        row_id == COLS - 1, right, pltpu.roll(n, COLS - 1, 0)
-                    ).astype(BF16)
+                row_step(r)
                 return carry
 
             return lax.fori_loop(0, ROWS + 2, step, carry, unroll=6)
@@ -266,6 +278,12 @@
     def flat(piece):
         return piece.reshape(-1, CH)
 
+    def conv_one_row(b):
+        total = acc1[...]
+        for c in range(3):
+            total = total + dot(flat(xs[c, 2:4, b : b + ROWS]), w1[18 + b * 3 + c])
+        acc1[...] = total
+
     def conv_one(a):
         total = acc1[...]
         for b in range(3):
@@ -283,26 +301,80 @@
             acce[q] += dot(flat(xs[2 * q, pl.ds(a, 2), 1 : 1 + ROWS]), we[a * 2 + q])
             accg[q] += dot(flat(xs[2 * q, pl.ds(a, 2)]), wg[a * 2 + q])
 
-    def norm_and_convolve(stage, conv, near, far):
-        def step(i, carry):
-            @pl.when(i == 0)
-            def _():
-                for copy in near:
-                    copy.wait_recv()
-
-            @pl.when(i == 1)
-            def _():
-                for copy in far:
-                    copy.wait_recv()
-
-            @pl.when(i < 2)
-            def _():
-                normalize(stage, 1 - i)
-
-            conv(2 - i)
-            return carry
-
-        lax.fori_loop(0, 3, step, 0)
+    def beside(products, work):
+        done = 0
+        for i, product in enumerate(products):
+            product()
+            until = (i + 1) * len(work) // len(products)
+            for n in range(done, until):
+                work[n]()
+            done = until
+
+    def rows_before(stage):
+        work = []
+        for f in range(2):
+            step = norm_rows(stage, f)
+            work += [functools.partial(step, r) for r in range(ROWS + 2)]
+        return work
+
+    def products_two(a):
+        def middle(p):
+            total = acc2[p]
+            for d in range(2):
+                total = total + dot(flat(xs[1, a : a + 2, p + d : p + d + ROWS]), wc[a * 4 + p * 2 + d])
+            acc2[p] = total
+
+        def inner(q):
+            acce[q] += dot(flat(xs[2 * q, a : a + 2, 1 : 1 + ROWS]), we[a * 2 + q])
+
+        def outer(q):
+            accg[q] += dot(flat(xs[2 * q, a : a + 2]), wg[a * 2 + q])
+
+        return [functools.partial(f, i) for f in (middle, inner, outer) for i in range(2)]
+
+    def chain_two():
+        def middle(p, f, frames):
+            place = slice(f * ROWS * COLS, (f + frames) * ROWS * COLS)
+            total = acc2[p, place]
+            for a in (1, 0):
+                for d in range(2):
+                    piece = xs[1, a + f : a + f + frames, p + d : p + d + ROWS]
+                    total = total + dot(flat(piece), wc[a * 4 + p * 2 + d])
+            acc2[p, place] = total
+
+        def outputs(p, f):
+            return [functools.partial(finish, p, f, i) for i in range(ROWS)]
+
+        for q in range(2):
+            total = acce[q]
+            for a in (1, 0):
+                total = total + dot(flat(xs[2 * q, a : a + 2, 1 : 1 + ROWS]), we[a * 2 + q])
+            acce[q] = total
+            total = accg[q]
+            for a in (1, 0):
+                total = total + dot(flat(xs[2 * q, a : a + 2]), wg[a * 2 + q])
+            accg[q] = total
+        middle(0, 0, 2)
+        middle(1, 0, 1)
+        for work in outputs(0, 0) + outputs(0, 1):
+            work()
+        middle(1, 1, 1)
+        for work in outputs(1, 0):
+            work()
+        pltpu.make_async_copy(ob.at[0], out.at[0], osem.at[0]).start()
+        for work in outputs(1, 1):
+            work()
+        pltpu.make_async_copy(ob.at[1], out.at[1], osem.at[1]).start()
+
+    def finish(p, f, i):
+        slot = i % 8
+        place = slice((f * ROWS + i) * COLS, (f * ROWS + i + 1) * COLS)
+        row = f * (ROWS + 2) + i + 2 * p
+        outer = slice(row * COLS, (row + 1) * COLS)
+        for q in range(2):
+            v = acc2[p, place, q * CO : (q + 1) * CO] + acce[q, place, p * CO : (p + 1) * CO]
+            tmp[slot, pl.ds(q, COLS, stride=2), :] = v + accg[q, outer, p * CO : (p + 1) * CO]
+        ob[f, i * 2 + p] = tmp[slot].astype(BF16)
 
     load_lat.wait()
     take_in(0, lambda f, r: buf[0, 2 + f, 1 + r].astype(F32))
@@ -316,7 +388,19 @@
     fold_weights()
     acc1[...] = jnp.zeros_like(acc1)
     end_line(0, prm[0], prm[1])
-    norm_and_convolve(0, conv_one, near, far)
+    for copy in near:
+        copy.wait_recv()
+    normalize(0, 1)
+    for copy in far:
+        copy.wait_recv()
+    norm_edges(0, 0)
+    beside([functools.partial(conv_one_row, b) for b in range(3)], rows_before(0))
+
+    def tap_step(i, carry):
+        conv_one(1 - i)
+        return carry
+
+    lax.fori_loop(0, 2, tap_step, 0)
 
     bias = jnp.concatenate([prm[2, 0:1], prm[2, 1:2]], axis=1)
 
@@ -330,31 +414,22 @@
     start_plane(1)
     edges(1)
     near, far = send_halo(1)
-    skip[...] = dot(buf[1, 2:4, 1 : ROWS + 1].reshape(2 * ROWS * COLS, CH), ws[...]) + b2[...]
     start_line(1)
-    acc2[...] = jnp.zeros_like(acc2)
+    skip = dot(flat(buf[1, 2:4, 1 : ROWS + 1]), ws[...]) + b2[...]
+    for p in range(2):
+        for q in range(2):
+            acc2[p, :, q * CO : (q + 1) * CO] = skip
     acce[...] = jnp.zeros_like(acce)
     accg[...] = jnp.zeros_like(accg)
     end_line(1, prm[3], prm[4])
-    norm_and_convolve(1, conv_two, near, far)
-
-    def finish(u, carry):
-        f = u // ROWS
-        i = lax.rem(u, ROWS)
-        place = pl.ds(pl.multiple_of(u * COLS, COLS), COLS)
-        extra = skip[place]
-        for p in range(2):
-            for q in range(2):
-                outer = pl.ds(pl.multiple_of((u + 2 * f + 2 * p) * COLS, COLS), COLS)
-                v = acc2[p, place, q * CO : (q + 1) * CO] + acce[q, place, p * CO : (p + 1) * CO]
-                v = v + (accg[q, outer, p * CO : (p + 1) * CO] + extra)
-                tmp[lax.rem(u, 2) * 2 + p, pl.ds(q, COLS, stride=2), :] = v
-            ob[f, i * 2 + p] = tmp[lax.rem(u, 2) * 2 + p].astype(BF16)
-        return carry
-
-    for f in range(2):
-        lax.fori_loop(f * ROWS, (f + 1) * ROWS, finish, 0, unroll=4)
-        pltpu.make_async_copy(ob.at[f], out.at[f], osem.at[f]).start()
+    for copy in near:
+        copy.wait_recv()
+    normalize(1, 1)
+    for copy in far:
+        copy.wait_recv()
+    norm_edges(1, 0)
+    beside(products_two(2), rows_before(1))
+    chain_two()
 
     for copy in sends:
         copy.wait_send()
@@ -401,8 +476,7 @@
             vmem((2, 2 * ROWS * COLS, 2 * CO), F32),
             vmem((2, 2 * ROWS * COLS, 2 * CO), F32),
             vmem((2, 2 * (ROWS + 2) * COLS, 2 * CO), F32),
-            vmem((2 * ROWS * COLS, CO), F32),
-            vmem((4, 2 * COLS, CO), F32),
+            vmem((8, 2 * COLS, CO), F32),
             vmem((2, 2 * ROWS, 2 * COLS, CO), BF16),
             vmem((2, 1, 128), F32),
             vmem((2, 1, 384), F32),

time: 40.3 us -> 39.1 us (0.970)
  Pallas kernels: 38.3 us -> 37.1 us
    pallas_call x1, Pallas kernels: 38.3 us -> 37.1 us  [on_device(): pl.pallas_call(kernel, out_shape=jax.ShapeDtypeStruct((2, 2 * ROWS, 2 * C...]
where the time goes in v3:
time: 39.1 us; the launch traced here: 38.9 us
  Pallas kernels  37.1 us (95%)
  local copies, waits for them, and re-layouts  1.87 us (5%)
    pallas_call x1, Pallas kernels, on_device(): pl.pallas_call(kernel, out_shape=jax.ShapeDtypeStruct((2, 2 * ROWS, 2 * C...  37.1 us
    unnamed x1, local copies, waits for them, and re-layouts  1.87 us

profile of v3, /device:TPU:1, one launch (start us, length us, event | category | flops | bytes accessed | tf_op | source)
XLA Modules:
  0.0 38.9 jit_solution(7241927769160435609)
XLA Ops:
  0.0 37.1 %shard_map.100 = bf16[2,32,32,128]{3,2,1,0:T(8,128)(2,1)} custom-call(bf16[2,16,16,256]{3,2,1,0:T(8,128)(2,1)} %lat.1, bf16[27,256,256]{2,1,0:T(8,128)(2,1)} %bitcast.8, bf16[27,256,128]{2,1,0:T(8,128)(2,1)} %bitcast.9, bf16[256,128]{1,0:T(8,128)(2,1)} %wsh.1, f32[2,128]{1,0:T(2,128)} %bitcast.10, f32[2,128]{1,0:T(2,128)} %bitcast.11, f32[2,128]{1,0:T(2,128)} %bitcast.12, ...), custom_call_target="tpu_custom_call" | custom-call | tf_op jit(solution)/shard_map/pallas_call | solution.py:450
  37.1 1.9 %copy.12 = bf16[2,32,32,128]{3,2,1,0:T(8,128)(2,1)} copy(bf16[2,32,32,128]{3,2,1,0:T(8,128)(2,1)} %shard_map.100) | data formatting | bytes 1048576

commit v4 on v3

--- a/solution.py
+++ b/solution.py
@@ -134,6 +134,9 @@
             copies.append(copy)
 
         copies = []
+        for f in (1, 0):
+            send(buf.at[stage, 2 + f, 1 : ROWS + 1], buf.at[stage, f, 1 : ROWS + 1], at(1, 0, 0))
+        edges(stage)
         for g, dt in ((1, 0), (0, 1)):
             for dy, dx, kind, a, b in PIECES:
                 device = at(dt, dy, dx)
@@ -143,12 +146,9 @@
                     send(colp.at[stage, a], colr.at[stage, g, b], device)
                 else:
                     send(cb.at[stage, a], cr.at[stage, g, b], device)
-            if g == 1:
-                for f in (1, 0):
-                    send(buf.at[stage, 2 + f, 1 : ROWS + 1], buf.at[stage, f, 1 : ROWS + 1], at(1, 0, 0))
         sends.extend(copies)
         near = len(PIECES)
-        return copies[:near], copies[near:]
+        return copies[2 : near + 2], copies[:2] + copies[near + 2 :]
 
     def start_plane(stage):
         msg[stage] = compact(sums[...])
@@ -249,7 +249,7 @@
                 row_step(r)
                 return carry
 
-            return lax.fori_loop(0, ROWS + 2, step, carry, unroll=6)
+            return lax.fori_loop(0, ROWS + 2, step, carry, unroll=9)
 
         lax.fori_loop(0, 2, frame_step, 0)
 
@@ -359,12 +359,15 @@
         for work in outputs(0, 0) + outputs(0, 1):
             work()
         middle(1, 1, 1)
-        for work in outputs(1, 0):
-            work()
-        pltpu.make_async_copy(ob.at[0], out.at[0], osem.at[0]).start()
-        for work in outputs(1, 1):
-            work()
-        pltpu.make_async_copy(ob.at[1], out.at[1], osem.at[1]).start()
+        for f in range(2):
+            for i, work in enumerate(outputs(1, f)):
+                work()
+                if i % 4 == 3:
+                    store(f, i // 4).start()
+
+    def store(f, part):
+        rows = pl.ds(part * 8, 8)
+        return pltpu.make_async_copy(ob.at[f, rows], out.at[f, rows], osem.at[f, part])
 
     def finish(p, f, i):
         slot = i % 8
@@ -380,7 +383,6 @@
     take_in(0, lambda f, r: buf[0, 2 + f, 1 + r].astype(F32))
     pl.semaphore_wait(ready, len(senders))
     start_plane(0)
-    edges(0)
     near, far = send_halo(0)
     for load in loads:
         load.wait()
@@ -412,7 +414,6 @@
 
     take_in(1, block_out)
     start_plane(1)
-    edges(1)
     near, far = send_halo(1)
     start_line(1)
     skip = dot(flat(buf[1, 2:4, 1 : ROWS + 1]), ws[...]) + b2[...]
@@ -437,7 +438,8 @@
         pltpu.make_async_copy(da.at[stage], da.at[stage], ssem_a.at[stage]).wait()
         pltpu.make_async_copy(db.at[stage], db.at[stage], ssem_b.at[stage]).wait()
     for f in range(2):
-        pltpu.make_async_copy(ob.at[f], out.at[f], osem.at[f]).wait()
+        for part in range(4):
+            store(f, part).wait()
 
 
 def on_device(
@@ -489,7 +491,7 @@
             dma((2,)),
             dma((2,)),
             dma((10,)),
-            dma((2,)),
+            dma((2, 4)),
         ],
         compiler_params=pltpu.CompilerParams(
             collective_id=0, has_side_effects=True, vmem_limit_bytes=62 << 20

time: 39.1 us -> 38.9 us (level)
  no operation moved by 1% of the time
where the time goes in v4:
time: 38.9 us; the launch traced here: 38.8 us
  Pallas kernels  36.9 us (95%)
  local copies, waits for them, and re-layouts  1.87 us (5%)
    pallas_call x1, Pallas kernels, on_device(): pl.pallas_call(kernel, out_shape=jax.ShapeDtypeStruct((2, 2 * ROWS, 2 * C...  36.9 us
    unnamed x1, local copies, waits for them, and re-layouts  1.87 us

profile of v4, /device:TPU:1, one launch (start us, length us, event | category | flops | bytes accessed | tf_op | source)
XLA Modules:
  0.0 38.8 jit_solution(10437761473780470870)
XLA Ops:
  0.0 36.9 %shard_map.100 = bf16[2,32,32,128]{3,2,1,0:T(8,128)(2,1)} custom-call(bf16[2,16,16,256]{3,2,1,0:T(8,128)(2,1)} %lat.1, bf16[27,256,256]{2,1,0:T(8,128)(2,1)} %bitcast.8, bf16[27,256,128]{2,1,0:T(8,128)(2,1)} %bitcast.9, bf16[256,128]{1,0:T(8,128)(2,1)} %wsh.1, f32[2,128]{1,0:T(2,128)} %bitcast.10, f32[2,128]{1,0:T(2,128)} %bitcast.11, f32[2,128]{1,0:T(2,128)} %bitcast.12, ...), custom_call_target="tpu_custom_call" | custom-call | tf_op jit(solution)/shard_map/pallas_call | solution.py:452
  36.9 1.9 %copy.12 = bf16[2,32,32,128]{3,2,1,0:T(8,128)(2,1)} copy(bf16[2,32,32,128]{3,2,1,0:T(8,128)(2,1)} %shard_map.100) | data formatting | bytes 1048576

commit v5 on v4

--- a/solution.py
+++ b/solution.py
@@ -39,9 +39,9 @@
 
 def kernel(
     lat, w1h, w2h, wsh, g1h, s1h, b1h, g2h, s2h, b2h, out,
-    buf, colp, colr, cb, cr, wide, xs, hal, sums, red, sc, w1, w2, wc, we, wg, ws, prm, b2,
+    buf, colp, colr, cb, cr, wide, xs, hal, sums, sc, w1, w2, wc, we, wg, ws, prm, b2,
     acc1, acc2, acce, accg, tmp, ob,
-    msg, msg3, da, db, ssem, rsem, ssem_a, rsem_a, ssem_b, rsem_b, lsem, osem,
+    msg, msg2, da, db, ssem, rsem, ssem_a, rsem_a, ssem_b, rsem_b, lsem, osem,
 ):
     t = lax.axis_index("ta")
     gy = lax.axis_index("gy")
@@ -167,37 +167,36 @@
             for k in range(1, NCHIP):
                 total = total + da[stage, j * NCHIP + k - 1]
             spans.append(total if j == 0 else jnp.where(t >= j, total, 0.0))
-        msg3[stage] = jnp.concatenate([spans[0], spans[1], spans[2] + spans[3]], axis=1)
+        second = (lane[0:1] & 2) != 0
+        up = [pltpu.roll(v, 2, 1) for v in (spans[0], spans[1], spans[2] + spans[3])]
+        own, before = [v + jnp.where(second, u, 0.0) for v, u in zip(spans[:2], up)]
+        pair = spans[1] + jnp.where(second, up[1], pltpu.roll(spans[1], 126, 1))
+        older = spans[2] + spans[3]
+        older = older + jnp.where(second, up[2], pltpu.roll(older, 126, 1))
+        msg2[stage] = jnp.concatenate([before + older, own + (pair + older)], axis=1)
         for i, (c, k) in enumerate(LINE):
             pltpu.make_async_remote_copy(
-                msg3.at[stage], db.at[stage, i], ssem_b.at[stage], rsem_b.at[stage],
+                msg2.at[stage], db.at[stage, i], ssem_b.at[stage], rsem_b.at[stage],
                 device_id=on_line(c, k), device_id_type=MESH,
             ).start()
 
     def end_line(stage, gain, shift):
         everything = db.at[stage]
         pltpu.make_async_copy(everything, everything, rsem_b.at[stage]).wait()
-        total = msg3[stage]
+        total = msg2[stage]
         for i in range(len(LINE)):
             total = total + db[stage, i]
-        for i in range(3):
-            red[i] = expand(total[:, i * 128 : i * 128 + 128])
-        running = []
-        for s in (0, 4):
-            before = red[2, s : s + 2] + red[2, s + 2 : s + 4]
-            row = []
-            for i in (1, 0):
-                for f in range(2):
-                    before = before + red[i, s + 2 * f : s + 2 * f + 2]
-                    row.append(before)
-            running.append(row)
-        for f in range(4):
-            count = jnp.maximum((2 * t + f - 1).astype(F32), 1.0) * AREA
-            mean = running[0][f] / count
-            var = running[1][f] / count - mean * mean
+        frame = lax.broadcasted_iota(jnp.int32, (4, 128), 0) // 2
+        gain = jnp.concatenate([gain, gain], axis=0)
+        shift = jnp.concatenate([shift, shift], axis=0)
+        for g in range(2):
+            running = expand(total[:, g * 128 : g * 128 + 128])
+            count = jnp.maximum((2 * t + (2 * g - 1) + frame).astype(F32), 1.0) * AREA
+            mean = running[0:4] / count
+            var = running[4:8] / count - mean * mean
             scale = lax.rsqrt(var + EPS) * gain
-            sc[0, 2 * f : 2 * f + 2] = scale
-            sc[1, 2 * f : 2 * f + 2] = shift - mean * scale
+            sc[0, 4 * g : 4 * g + 4] = scale
+            sc[1, 4 * g : 4 * g + 4] = shift - mean * scale
 
     def silu(a):
         return 0.5 * a * (1.0 + jnp.tanh(0.5 * a))
@@ -342,9 +341,6 @@
                     total = total + dot(flat(piece), wc[a * 4 + p * 2 + d])
             acc2[p, place] = total
 
-        def outputs(p, f):
-            return [functools.partial(finish, p, f, i) for i in range(ROWS)]
-
         for q in range(2):
             total = acce[q]
             for a in (1, 0):
@@ -355,25 +351,25 @@
                 total = total + dot(flat(xs[2 * q, a : a + 2]), wg[a * 2 + q])
             accg[q] = total
         middle(0, 0, 2)
-        middle(1, 0, 1)
-        for work in outputs(0, 0) + outputs(0, 1):
-            work()
-        middle(1, 1, 1)
-        for f in range(2):
-            for i, work in enumerate(outputs(1, f)):
-                work()
-                if i % 4 == 3:
-                    store(f, i // 4).start()
+        middle(1, 0, 2)
+
+        def step(u, carry):
+            f, part = u // 4, lax.rem(u, 4)
+            for n in range(4):
+                for p in range(2):
+                    finish(p, f, part * 4 + n, 2 * n + p)
+            store(f, part).start()
+            return carry
+
+        lax.fori_loop(0, 8, step, 0)
 
     def store(f, part):
         rows = pl.ds(part * 8, 8)
         return pltpu.make_async_copy(ob.at[f, rows], out.at[f, rows], osem.at[f, part])
 
-    def finish(p, f, i):
-        slot = i % 8
-        place = slice((f * ROWS + i) * COLS, (f * ROWS + i + 1) * COLS)
-        row = f * (ROWS + 2) + i + 2 * p
-        outer = slice(row * COLS, (row + 1) * COLS)
+    def finish(p, f, i, slot):
+        place = pl.ds(pl.multiple_of((f * ROWS + i) * COLS, COLS), COLS)
+        outer = pl.ds(pl.multiple_of((f * (ROWS + 2) + i + 2 * p) * COLS, COLS), COLS)
         for q in range(2):
             v = acc2[p, place, q * CO : (q + 1) * CO] + acce[q, place, p * CO : (p + 1) * CO]
             tmp[slot, pl.ds(q, COLS, stride=2), :] = v + accg[q, outer, p * CO : (p + 1) * CO]
@@ -464,7 +460,6 @@
             vmem((3, 4, ROWS + 2, COLS, CH), BF16),
             vmem((2, 8 * 32, 128), F32),
             vmem((8, 128), F32),
-            vmem((3, 8, 128), F32),
             vmem((2, 8, 128), F32),
             vmem((27, CH, CH), BF16),
             vmem((27, CH, CO), BF16),
@@ -481,9 +476,9 @@
             vmem((8, 2 * COLS, CO), F32),
             vmem((2, 2 * ROWS, 2 * COLS, CO), BF16),
             vmem((2, 1, 128), F32),
-            vmem((2, 1, 384), F32),
+            vmem((2, 1, 256), F32),
             vmem((2, len(PLANE), 1, 128), F32),
-            vmem((2, len(LINE), 1, 384), F32),
+            vmem((2, len(LINE), 1, 256), F32),
             dma((2, n_halo)),
             dma((2, n_halo)),
             dma((2,)),

time: 38.9 us -> 39 us (level)
  no operation moved by 1% of the time
where the time goes in v5:
time: 39 us; the launch traced here: 38.8 us
  Pallas kernels  37 us (95%)
  local copies, waits for them, and re-layouts  1.87 us (5%)
    pallas_call x1, Pallas kernels, on_device(): pl.pallas_call(kernel, out_shape=jax.ShapeDtypeStruct((2, 2 * ROWS, 2 * C...  37 us
    unnamed x1, local copies, waits for them, and re-layouts  1.87 us

profile of v5, /device:TPU:1, one launch (start us, length us, event | category | flops | bytes accessed | tf_op | source)
XLA Modules:
  0.0 38.8 jit_solution(11146890605646039385)
XLA Ops:
  0.0 37.0 %shard_map.100 = bf16[2,32,32,128]{3,2,1,0:T(8,128)(2,1)} custom-call(bf16[2,16,16,256]{3,2,1,0:T(8,128)(2,1)} %lat.1, bf16[27,256,256]{2,1,0:T(8,128)(2,1)} %bitcast.8, bf16[27,256,128]{2,1,0:T(8,128)(2,1)} %bitcast.9, bf16[256,128]{1,0:T(8,128)(2,1)} %wsh.1, f32[2,128]{1,0:T(2,128)} %bitcast.10, f32[2,128]{1,0:T(2,128)} %bitcast.11, f32[2,128]{1,0:T(2,128)} %bitcast.12, ...), custom_call_target="tpu_custom_call" | custom-call | tf_op jit(solution)/shard_map/pallas_call | solution.py:448
  37.0 1.9 %copy.12 = bf16[2,32,32,128]{3,2,1,0:T(8,128)(2,1)} copy(bf16[2,32,32,128]{3,2,1,0:T(8,128)(2,1)} %shard_map.100) | data formatting | bytes 1048576

commit v6 on v4

--- a/solution.py
+++ b/solution.py
@@ -102,7 +102,7 @@
                 return s + v, q + v * v
 
             zero = jnp.zeros((COLS, CH), F32)
-            s, q = lax.fori_loop(0, ROWS, step, (zero, zero), unroll=4)
+            s, q = lax.fori_loop(0, ROWS, step, (zero, zero), unroll=8)
             s = jnp.sum(s, axis=0, keepdims=True)
             q = jnp.sum(q, axis=0, keepdims=True)
             for h in range(2):

time: 38.9 us -> 38.9 us (level)
  no operation moved by 1% of the time
where the time goes in v6:
time: 38.9 us; the launch traced here: 38.8 us
  Pallas kernels  36.9 us (95%)
  local copies, waits for them, and re-layouts  1.87 us (5%)
    pallas_call x1, Pallas kernels, on_device(): pl.pallas_call(kernel, out_shape=jax.ShapeDtypeStruct((2, 2 * ROWS, 2 * C...  36.9 us
    unnamed x1, local copies, waits for them, and re-layouts  1.87 us

profile of v6, /device:TPU:1, one launch (start us, length us, event | category | flops | bytes accessed | tf_op | source)
XLA Modules:
  0.0 38.8 jit_solution(18188643441356678831)
XLA Ops:
  0.0 36.9 %shard_map.100 = bf16[2,32,32,128]{3,2,1,0:T(8,128)(2,1)} custom-call(bf16[2,16,16,256]{3,2,1,0:T(8,128)(2,1)} %lat.1, bf16[27,256,256]{2,1,0:T(8,128)(2,1)} %bitcast.8, bf16[27,256,128]{2,1,0:T(8,128)(2,1)} %bitcast.9, bf16[256,128]{1,0:T(8,128)(2,1)} %wsh.1, f32[2,128]{1,0:T(2,128)} %bitcast.10, f32[2,128]{1,0:T(2,128)} %bitcast.11, f32[2,128]{1,0:T(2,128)} %bitcast.12, ...), custom_call_target="tpu_custom_call" | custom-call | tf_op jit(solution)/shard_map/pallas_call | solution.py:452
  36.9 1.9 %copy.12 = bf16[2,32,32,128]{3,2,1,0:T(8,128)(2,1)} copy(bf16[2,32,32,128]{3,2,1,0:T(8,128)(2,1)} %shard_map.100) | data formatting | bytes 1048576
